TPU v7x, 256 devices: a whole 4x4x8 slice. The times are simulated.
256 devices in a mesh: row: 16 (over x, z_hi), col: 16 (over y, z_lo, core).
Axes of the slice: x: 4, y: 4, z: 8 (z_hi: 4, z_lo: 2; z = z_hi * 2 + z_lo), core: 2. Of those that a mesh axis runs over, the one named last changes fastest.
Arguments:
- pair: bfloat16 [640, 640, 128], P('row', 'col'), may hold values from -6 to 6
- token_mask: int32 [640], replicated, may hold values from 0 to 1, as said below
- chain_ids: int32 [640], replicated, may hold values from 0 to 7, never falling along the last dimension, each value on 1 to 160 neighbouring positions
- chain_bias: float32 [128], replicated, may hold values from -4 to 4
- in_weights: bfloat16 [2, 128, 640], replicated, may hold values from -0.5 to 0.5
- out_weights: bfloat16 [2, 128, 128], replicated, may hold values from -0.5 to 0.5
Outputs:
- pair_out: bfloat16 [640, 640, 128], P('row', 'col')
Inputs may be any that keep to these rules, and one draw needn't show every extreme that they name: token_mask is 0 on a run of padding at the end that always includes the last token; some tokens before it may be 0 as well. chain_ids never falls along the tokens.
All inputs are finite; a program needn't handle non-finite values.
Results may differ from a plain program's by a relative error of at most 0.015.
Values may be sent and summed in bfloat16 or wider, within the bound.
A program may use at most 128 MiB of HBM per device.

v0:
```python
import jax
import jax.numpy as jnp
from jax import lax
from jax.sharding import PartitionSpec as P


def layer_norm(values):
    center = values - jnp.mean(values, axis=-1, keepdims=True)
    spread = jnp.mean(center * center, axis=-1, keepdims=True)
    return center * lax.rsqrt(spread + 1e-05)


def gated_inputs(field, weights, pair_mask):
    width = weights.shape[0]
    normed = layer_norm(field).astype(jnp.bfloat16)
    projected = jnp.einsum("ijc,cd->ijd", normed, weights, preferred_element_type=jnp.float32)
    first = (
        jax.nn.sigmoid(projected[..., :width])
        * projected[..., width : 2 * width]
        * pair_mask[:, :, None]
    ).astype(jnp.bfloat16)
    second = (
        jax.nn.sigmoid(projected[..., 2 * width : 3 * width])
        * projected[..., 3 * width : 4 * width]
        * pair_mask[:, :, None]
    ).astype(jnp.bfloat16)
    gate_value = jax.nn.sigmoid(projected[..., 4 * width :])
    return (first, second, gate_value)


def update(field, summed, gate_value, weights):
    normed_sum = layer_norm(summed).astype(jnp.bfloat16)
    output = jnp.einsum("ijc,cd->ijd", normed_sum, weights, preferred_element_type=jnp.float32)
    return field + gate_value * output


def per_device(pair, token_mask, chain_ids, chain_bias, in_weights, out_weights):
    row_count = pair.shape[0]
    col_count = pair.shape[1]
    row_start = lax.axis_index("row") * row_count
    col_start = lax.axis_index("col") * col_count
    valid_rows = lax.dynamic_slice_in_dim(token_mask, row_start, row_count).astype(jnp.float32)
    valid_cols = lax.dynamic_slice_in_dim(token_mask, col_start, col_count).astype(jnp.float32)
    chain_rows = lax.dynamic_slice_in_dim(chain_ids, row_start, row_count)
    chain_cols = lax.dynamic_slice_in_dim(chain_ids, col_start, col_count)
    pair_mask = valid_rows[:, None] * valid_cols[None, :]
    same_chain = (chain_rows[:, None] == chain_cols[None, :]).astype(jnp.float32)
    field = pair.astype(jnp.float32) + same_chain[:, :, None] * chain_bias
    first, second, gate_value = gated_inputs(field, in_weights[0], pair_mask)
    second_rows = lax.all_gather(second, "row", axis=0, tiled=True)
    block = second_rows
    summed = lax.psum_scatter(
        jnp.einsum("jkc,ikc->jic", block, first, preferred_element_type=jnp.float32).astype(
            jnp.bfloat16
        ),
        "col",
        scatter_dimension=0,
        tiled=True,
    ).astype(jnp.float32)
    summed = jnp.transpose(summed, (1, 0, 2))
    field = update(field, summed, gate_value, out_weights[0])
    first, second, gate_value = gated_inputs(field, in_weights[1], pair_mask)
    first_cols = lax.all_gather(first, "col", axis=1, tiled=True)
    block = first_cols
    summed = lax.psum_scatter(
        jnp.einsum("kic,kjc->ijc", block, second, preferred_element_type=jnp.float32).astype(
            jnp.bfloat16
        ),
        "row",
        scatter_dimension=0,
        tiled=True,
    ).astype(jnp.float32)
    field = update(field, summed, gate_value, out_weights[1])
    return field.astype(jnp.bfloat16)


def solution(mesh):
    return jax.shard_map(
        per_device,
        mesh=mesh,
        in_specs=(P("row", "col", None), P(), P(), P(), P(), P()),
        out_specs=P("row", "col", None),
        check_vma=False,
    )
```

profile of v0, /device:TPU:1, one launch (start us, length us, event | category | flops | bytes accessed | tf_op | source)
XLA Modules:
  0.0 465.2 jit_solution(138049122221778854)
XLA Ops:
  7.5 1.5 fusion.40
  9.0 1.7 multiply_reduce_fusion.1
  10.8 2.5 fusion.41
  13.4 2.0 copy-done.1
  15.4 1.2 fusion.23
  16.7 1.5 copy.43
  18.2 93.4 %all-gather.3.cloned.1.call-done = bf16[640,40,128]{2,1,0:T(8,128)(2,1)} async-done(((bf16[40,40,128]{2,1,0:T(8,128)(2,1)}), bf16[640,40,128]{2,1,0:T(8,128)(2,1)}) %all-gather.3.cloned.1.call-update) | async-done | bytes 6553616 | tf_op jit(solution)/shard_map/all_gather | solution.py:50
  111.6 28.6 %copy.44 = bf16[640,40,128]{1,0,2:T(8,128)(2,1)} copy(bf16[640,40,128]{2,1,0:T(8,128)(2,1)} %all-gather.3.cloned.1.call-done) | data formatting | bytes 13107200 | tf_op jit(solution)/shard_map/all_gather | solution.py:50
  140.2 14.3 %fusion = bf16[640,40,128]{0,1,2:T(8,128)(2,1)} fusion(bf16[40,40,128]{1,0,2:T(8,128)(2,1)S(1)} %copy.43, bf16[640,40,128]{1,0,2:T(8,128)(2,1)} %copy.44), kind=kOutput, calls=%fused_computation.2 | convolution fusion | flops 265420800 | bytes 13516800 | tf_op jit(solution)/shard_map/jkc,ikc->jic/dot_general | solution.py:53
  154.6 11.6 %copy.45 = bf16[640,40,128]{2,1,0:T(8,128)(2,1)} copy(bf16[640,40,128]{0,1,2:T(8,128)(2,1)} %fusion) | data formatting | bytes 13107200 | tf_op jit(solution)/shard_map/convert_element_type | solution.py:53
  166.2 87.0 %reduce-scatter.3.cloned.1.call-done = bf16[40,40,128]{2,1,0:T(8,128)(2,1)} async-done(((bf16[640,40,128]{2,1,0:T(8,128)(2,1)}), bf16[40,40,128]{2,1,0:T(8,128)(2,1)}) %reduce-scatter.3.cloned.1.call-update) | async-done | bytes 409616 | tf_op jit(solution)/shard_map/reduce_scatter | solution.py:52
  253.2 1.3 bitcast_reduce_fusion
  254.6 1.5 fusion.37
  256.3 1.5 fusion.38
  257.9 1.8 fusion.62
  261.3 1.9 copy-done
  265.9 45.7 %all-gather.5.cloned.1.call-done = bf16[40,640,128]{2,1,0:T(8,128)(2,1)} async-done(((bf16[40,40,128]{2,1,0:T(8,128)(2,1)}), bf16[40,640,128]{2,1,0:T(8,128)(2,1)}) %all-gather.5.cloned.1.call-update) | async-done | bytes 6553616 | tf_op jit(solution)/shard_map/all_gather | solution.py:63
  311.7 10.8 %copy.52 = bf16[40,640,128]{1,0,2:T(8,128)(2,1)} copy(bf16[40,640,128]{2,1,0:T(8,128)(2,1)} %all-gather.5.cloned.1.call-done) | data formatting | bytes 13107200 | tf_op jit(solution)/shard_map/all_gather | solution.py:63
  322.5 7.8 %fusion.1 = bf16[640,40,128]{0,1,2:T(8,128)(2,1)} fusion(bf16[40,40,128]{0,1,2:T(8,128)(2,1)S(1)} %copy.51, bf16[40,640,128]{1,0,2:T(8,128)(2,1)} %copy.52), kind=kOutput, calls=%fused_computation.3 | convolution fusion | flops 265420800 | bytes 13516800 | tf_op jit(solution)/shard_map/kic,kjc->ijc/dot_general | solution.py:66
  330.2 11.6 %copy.53 = bf16[640,40,128]{2,1,0:T(8,128)(2,1)} copy(bf16[640,40,128]{0,1,2:T(8,128)(2,1)} %fusion.1) | data formatting | bytes 13107200 | tf_op jit(solution)/shard_map/convert_element_type | solution.py:66
  341.8 111.3 %reduce-scatter.5.cloned.1.call-done = bf16[40,40,128]{2,1,0:T(8,128)(2,1)} async-done(((bf16[640,40,128]{2,1,0:T(8,128)(2,1)}), bf16[40,40,128]{2,1,0:T(8,128)(2,1)}) %reduce-scatter.5.cloned.1.call-update) | async-done | bytes 409616 | tf_op jit(solution)/shard_map/reduce_scatter | solution.py:65
  453.1 1.3 convert_reduce_fusion
  454.4 1.5 fusion.7
  455.9 2.7 fusion.4
  (37 shorter events, 5.8 us)
Async XLA Ops:
  6.5 105.1 %all-gather.3.cloned.1.call-start = ((), (), s32[]{:S(2)}) async-start(), calls=%async_computation.2 | async-start | bytes 6963200 | tf_op jit(solution)/shard_map/all_gather | solution.py:50
  13.4 2.0 copy-start.1
  16.7 236.5 %reduce-scatter.3.cloned.1.call-start = ((), (), s32[]{:S(2)}) async-start(), calls=%async_computation.3 | async-start | bytes 6963200 | tf_op jit(solution)/shard_map/reduce_scatter | solution.py:52
  166.1 91.7 %copy-start.2 = (bf16[40,40,128]{2,1,0:T(8,128)(2,1)S(1)}, bf16[40,40,128]{2,1,0:T(8,128)(2,1)}, u32[]{:S(2)}) copy-start(bf16[40,40,128]{2,1,0:T(8,128)(2,1)} %param.6) | copy-start | bytes 1228804
  166.1 91.7 %copy-start.4 = (f32[128]{0:T(128)S(1)}, f32[128]{0:T(128)}, u32[]{:S(2)}) copy-start(f32[128]{0:T(128)} %param.9) | copy-start | bytes 1540
  166.1 91.7 %copy-start.5 = (bf16[2,128,128]{2,1,0:T(8,128)(2,1)S(1)}, bf16[2,128,128]{2,1,0:T(8,128)(2,1)}, u32[]{:S(2)}) copy-start(bf16[2,128,128]{2,1,0:T(8,128)(2,1)} %param.11) | copy-start | bytes 196612
  166.1 94.1 %copy-start.3 = (bf16[2,128,640]{2,1,0:T(8,128)(2,1)S(1)}, bf16[2,128,640]{2,1,0:T(8,128)(2,1)}, u32[]{:S(2)}) copy-start(bf16[2,128,640]{2,1,0:T(8,128)(2,1)} %param.10) | copy-start | bytes 983044
  166.2 145.5 %all-gather.5.cloned.1.call-start = ((), (), s32[]{:S(2)}) async-start(), calls=%async_computation.4 | async-start | bytes 6963200 | tf_op jit(solution)/shard_map/all_gather | solution.py:63
  261.3 1.9 copy-start
  264.5 188.6 %reduce-scatter.5.cloned.1.call-start = ((), (), s32[]{:S(2)}) async-start(), calls=%async_computation.5 | async-start | bytes 6963200 | tf_op jit(solution)/shard_map/reduce_scatter | solution.py:65
Sparse Core Ops, SparseCore 0:
  16.8 94.7 all-gather.2
  166.3 86.8 reduce-scatter.2
  264.6 47.0 all-gather.4
  341.9 111.1 reduce-scatter.4
where the time goes:
time: 466 us; the launch traced here: 465 us
  waiting for transfers between devices  337 us (72%)
  local copies, waits for them, and re-layouts  69.5 us (15%)
  matrix products  30.1 us (6%)
  other arithmetic  14.4 us (3%)
  between operations  13.3 us (3%)
    reduce_scatter x1, waiting for transfers between devices, per_device(): lax.psum_scatter(jnp.einsum('kic,kjc->ijc', block, second, preferred_elem...  111 us
    all_gather x1, waiting for transfers between devices, per_device(): second_rows = lax.all_gather(second, 'row', axis=0, tiled=True)  93.4 us
    reduce_scatter x1, waiting for transfers between devices, per_device(): lax.psum_scatter(jnp.einsum('jkc,ikc->jic', block, first, preferred_eleme...  87 us
    all_gather x1, waiting for transfers between devices, per_device(): first_cols = lax.all_gather(first, 'col', axis=1, tiled=True)  45.7 us
    all_gather x1, local copies, waits for them, and re-layouts, per_device(): second_rows = lax.all_gather(second, 'row', axis=0, tiled=True)  28.6 us
    dot_general x1, matrix products, per_device(): jnp.einsum('jkc,ikc->jic', block, first, preferred_element_type=jnp.float32)  14.3 us
    convert_element_type x1, local copies, waits for them, and re-layouts, per_device(): jnp.einsum('jkc,ikc->jic', block, first, preferred_element_type=jnp.float32)  11.6 us
    convert_element_type x1, local copies, waits for them, and re-layouts, per_device(): jnp.einsum('kic,kjc->ijc', block, second, preferred_element_type=jnp.floa...  11.6 us
  transfers between devices with their start and end apart: 4, of which 4 were waited for; matrix products, arithmetic and copies ran while one was open for 1% of the time, Pallas kernels for 0%

commit v1 on v0

v1 whole, which is shorter than its diff:
```python
import functools

import jax
import jax.numpy as jnp
from jax import lax
from jax.experimental import pallas as pl
from jax.experimental.pallas import tpu as pltpu
from jax.sharding import PartitionSpec as P


MESH = pl.DeviceIdType.MESH
TOK = 40
ROWS = 16
PLANE = 8
CHIPS = ROWS * PLANE
CH = 128
PERM = 16 * 128
BF = jnp.bfloat16
F32 = jnp.float32
VMEM_LIMIT = 40 * 2**20


def sigmoid(x):
    return 0.5 * jnp.tanh(0.5 * x) + 0.5


def norm_lanes(x):
    center = x - jnp.mean(x, axis=-1, keepdims=True)
    spread = jnp.mean(center * center, axis=-1, keepdims=True)
    return center * lax.rsqrt(spread + 1e-05)


def start_field(pair_ref, chain_rows_ref, chain_cols_ref, bias_ref, field_ref):
    bias = bias_ref[...]
    cols = chain_cols_ref[...]
    for i in range(TOK):
        same = cols == chain_rows_ref[i]
        field_ref[pl.ds(i * TOK, TOK)] = pair_ref[i].astype(F32) + jnp.where(same, bias, 0.0)


def produce(field_ref, w_ref, mask_ref, f_ref, s_ref, gate_ref, nat, perm, tiles, swap):
    nat[...] = norm_lanes(field_ref[...])
    for g in range(16):
        for q in range(3):
            a = 16 * q + g
            at = pl.ds(g * 128 + TOK * q, TOK)
            if a >= TOK:
                perm[at] = jnp.zeros((TOK, CH), F32)
            elif swap:
                perm[at] = nat[pl.ds(a, TOK, stride=TOK)]
            else:
                perm[at] = nat[pl.ds(a * TOK, TOK)]
        perm[pl.ds(g * 128 + 120, 8)] = jnp.zeros((8, CH), F32)
    weights_t = jnp.transpose(w_ref[...].astype(F32)).astype(BF)
    for half, out in enumerate((f_ref, s_ref)):
        for part in range(4):
            lo = part * 512
            normed = perm[pl.ds(lo, 512)].astype(BF)
            both = lax.dot_general(
                weights_t[half * 256 : half * 256 + 256], normed, (((1,), (1,)), ((), ())), preferred_element_type=F32
            )
            value = sigmoid(both[:CH]) * both[CH:]
            for n in range(4):
                g = part * 4 + n
                tiles[pl.ds(g, CH, stride=16)] = value[:, n * 128 : n * 128 + 128] * mask_ref[g : g + 1, :]
        out[...] = tiles[...].reshape(CH, 16, 128).astype(BF)
    for part in range(4):
        normed = perm[pl.ds(part * 512, 512)].astype(BF)
        value = sigmoid(jnp.dot(normed, w_ref[:, 512:640], preferred_element_type=F32))
        for n in range(4):
            for q in range(3):
                a = 16 * q + part * 4 + n
                if a < TOK:
                    piece = value[n * 128 + q * TOK : n * 128 + q * TOK + TOK]
                    if swap:
                        gate_ref[pl.ds(a, TOK, stride=TOK)] = piece
                    else:
                        gate_ref[pl.ds(a * TOK, TOK)] = piece


def finish(field_ref, gate_ref, r_ref, w_ref, tiles):
    x = r_ref[...].astype(F32)
    center = x - jnp.mean(x, axis=0, keepdims=True)
    spread = jnp.mean(center * center, axis=0, keepdims=True)
    tiles[...] = (center * lax.rsqrt(spread + 1e-05)).reshape(CH * 16, 128)
    weights = w_ref[...]
    for g in range(16):
        normed = tiles[pl.ds(g, CH, stride=16)].astype(BF)
        out = lax.dot_general(normed, weights, (((0,), (0,)), ((), ())), preferred_element_type=F32)
        for q in range(3):
            a = 16 * q + g
            if a < TOK:
                at = pl.ds(a * TOK, TOK)
                field_ref[at] = field_ref[at] + gate_ref[at] * out[q * TOK : q * TOK + TOK]


def lanes_between(lo, hi, rows):
    lane = lax.broadcasted_iota(jnp.int32, (rows, 128), 1)
    return (lane >= lo) & (lane < hi)


def roll(x, amount):
    amount = amount % 128
    return pltpu.roll(x, amount, 1) if amount else x


def spread_lanes(blocks, q, rows):
    total = jnp.zeros((rows, 128), F32)
    for m, block in enumerate(blocks):
        total = jnp.where(lanes_between(TOK * m, TOK * m + TOK, rows), roll(block, TOK * (m - q)), total)
    return total


def triangle(load_m, load_n, out_ref, left, right, part):
    part[...] = jnp.zeros((384, 128), F32)
    for group in range(6):
        blocks = range(3 * group, min(3 * group + 3, 16))
        lane = pl.ds(group * 128, 128)
        m_blocks = [load_m(k).astype(F32) for k in blocks]
        n_blocks = [load_n(k).astype(F32) for k in blocks]
        for q in range(3):
            left[pl.ds(q * 256, 256), lane] = spread_lanes(m_blocks, q, 256).astype(BF)
            value = spread_lanes(n_blocks, q, 128)
            for n in range(8):
                depth = 16 if q < 2 else 8
                part[pl.ds(128 * (n // 3) + TOK * (n % 3) + 16 * q, depth)] = value[n * 16 : n * 16 + depth]
        right[:, lane] = part[...].astype(BF)
    for n3 in range(3):
        total = lax.dot_general(
            left[...], right[pl.ds(n3 * 128, 128)], (((1,), (1,)), ((), ())), preferred_element_type=F32
        )
        for m in range(3 if n3 < 2 else 2):
            value = jnp.zeros((256, 128), F32)
            for q in range(3):
                value = jnp.where(
                    lanes_between(TOK * q, TOK * q + TOK, 256),
                    roll(total[q * 256 : q * 256 + 256], TOK * (q - m)),
                    value,
                )
            out_ref[3 * n3 + m] = value.reshape(16, 16, 128).astype(BF)


def place():
    row, col = lax.axis_index("row"), lax.axis_index("col")
    return row, col // 2, col % 2


def enter(sibling):
    row, chip, core = place()
    barrier = pltpu.get_barrier_semaphore()

    def signal(step, carry):
        to_row = (row + step // PLANE) % ROWS
        to_chip = (chip + step % PLANE) % PLANE
        pl.semaphore_signal(barrier, inc=1, device_id=(to_row, to_chip * 2 + core), device_id_type=MESH)
        return carry

    lax.fori_loop(1, CHIPS, signal, 0)
    if sibling:
        pl.semaphore_signal(barrier, inc=1, device_id=(row, chip * 2 + 1 - core), device_id_type=MESH)
    pl.semaphore_wait(barrier, CHIPS if sibling else CHIPS - 1)


def send_all(src, dst, send_sem, recv_sem):
    row, chip, core = place()
    pltpu.make_async_copy(src(row, chip), dst, recv_sem).start()

    def send(step, carry):
        to_row = (row + step // PLANE) % ROWS
        to_chip = (chip + step % PLANE) % PLANE
        pltpu.make_async_remote_copy(
            src_ref=src(to_row, to_chip),
            dst_ref=dst,
            send_sem=send_sem,
            recv_sem=recv_sem,
            device_id=(to_row, to_chip * 2 + core),
            device_id_type=MESH,
        ).start()
        return carry

    lax.fori_loop(1, CHIPS, send, 0)


def wait_bytes(ref, sem):
    pltpu.make_async_copy(ref, ref, sem).wait()


def to_sibling(ref, send_sem, recv_sem):
    row, chip, core = place()
    copy = pltpu.make_async_remote_copy(
        src_ref=ref,
        dst_ref=ref,
        send_sem=send_sem,
        recv_sem=recv_sem,
        device_id=(row, chip * 2 + 1 - core),
        device_id_type=MESH,
    )
    copy.start()
    return copy


def scatter_out(f_ref, s_ref, rf, rs, f_send, f_recv, s_send, s_recv, on_send, on_recv):
    row, chip, core = place()
    enter(True)
    index = row * PLANE + chip
    send_all(lambda r, c: f_ref.at[r * PLANE + c], rf.at[core, chip, row], f_send, f_recv)
    send_all(
        lambda r, c: s_ref.at[r * PLANE + c], rs.at[row % 2, core, chip, row // 2], s_send, s_recv.at[row % 2]
    )
    wait_bytes(rf.at[0], f_recv)
    copy_f = to_sibling(rf.at[core], on_send.at[0], on_recv.at[0])
    wait_bytes(rs.at[0, 0], s_recv.at[1 - core])
    copy_s = to_sibling(rs.at[1 - core, core], on_send.at[1], on_recv.at[1])
    wait_bytes(rs.at[0, 0], s_recv.at[core])
    copy_f.wait()
    copy_s.wait()
    wait_bytes(f_ref.at[pl.ds(0, CHIPS - 1)], f_send)
    wait_bytes(f_ref.at[pl.ds(0, CHIPS - 1)], s_send)


def scatter_in(f_ref, s_ref, rf, rs, f_send, f_recv, s_send, s_recv, on_send, on_recv):
    row, chip, core = place()
    enter(True)
    send_all(lambda r, c: f_ref.at[r * PLANE + c], rf.at[core, row, chip], f_send, f_recv)
    send_all(lambda r, c: s_ref.at[r * PLANE + c], rs.at[row, chip], s_send, s_recv)
    wait_bytes(rf.at[0], f_recv)
    copy_f = to_sibling(rf.at[core], on_send, on_recv)
    wait_bytes(rs, s_recv)
    copy_f.wait()
    wait_bytes(f_ref.at[pl.ds(0, CHIPS - 1)], f_send)
    wait_bytes(f_ref.at[pl.ds(0, CHIPS - 1)], s_send)


def bring_back(incoming, o_ref, r_ref, send_sem, recv_sem):
    row, chip, core = place()
    enter(False)
    if incoming:
        src = lambda r, c: o_ref.at[c, (r % 2) * PLANE + r // 2]
    else:
        src = lambda r, c: o_ref.at[c, r]
    send_all(src, r_ref.at[row * PLANE + chip], send_sem, recv_sem)
    wait_bytes(r_ref, recv_sem)
    wait_bytes(r_ref.at[pl.ds(0, CHIPS - 1)], send_sem)


def first_kernel(pair_ref, rows_ref, cols_ref, bias_ref, w_ref, mask_ref, f_ref, s_ref, gate_ref, field_ref, nat, perm, tiles):
    start_field(pair_ref, rows_ref, cols_ref, bias_ref, field_ref)
    produce(field_ref, w_ref, mask_ref, f_ref, s_ref, gate_ref, nat, perm, tiles, False)


def middle_kernel(
    field_ref, gate_ref, r_ref, wo_ref, w_ref, mask_ref, f_ref, s_ref, gate2_ref, field2_ref, nat, perm, tiles
):
    field2_ref[...] = field_ref[...]
    finish(field2_ref, gate_ref, r_ref, wo_ref, tiles)
    produce(field2_ref, w_ref, mask_ref, f_ref, s_ref, gate2_ref, nat, perm, tiles, True)


def last_kernel(field_ref, gate_ref, r_ref, wo_ref, out_ref, field2, tiles):
    field2[...] = field_ref[...]
    finish(field2, gate_ref, r_ref, wo_ref, tiles)
    for i in range(TOK):
        out_ref[i] = field2[pl.ds(i * TOK, TOK)].astype(BF)


def triangle_out_kernel(rf, rs, o_ref, left, right, part):
    core = lax.axis_index("col") % 2
    triangle(
        lambda k: rf[k % 2, k // 2].reshape(256, 128),
        lambda k: rs[core, k % 2, k // 2].reshape(128, 128),
        o_ref,
        left,
        right,
        part,
    )


def triangle_in_kernel(rf, rs, o_ref, left, right, part):
    triangle(
        lambda k: jnp.concatenate([rf[0, k], rf[1, k]], axis=0).reshape(256, 128),
        lambda k: rs[k].reshape(128, 128),
        o_ref,
        left,
        right,
        part,
    )


def call(kernel, outs, args, scratch, name, collective=None, smem=()):
    outs = [jax.ShapeDtypeStruct(shape, dtype) for shape, dtype in outs]
    params = dict(vmem_limit_bytes=VMEM_LIMIT)
    if collective is not None:
        params.update(collective_id=collective, has_side_effects=True)
    return pl.pallas_call(
        kernel,
        out_shape=outs,
        in_specs=[
            pl.BlockSpec(memory_space=pltpu.SMEM if i in smem else pltpu.VMEM) for i in range(len(args))
        ],
        out_specs=[pl.BlockSpec(memory_space=pltpu.VMEM)] * len(outs),
        scratch_shapes=scratch,
        compiler_params=pltpu.CompilerParams(**params),
        name=name,
    )(*args)


def tile_mask(a_valid, b_valid):
    a = jnp.pad(a_valid, (0, 8)).reshape(3, 16).T
    return jnp.pad((a[:, :, None] * b_valid[None, None, :]).reshape(16, 120), ((0, 0), (0, 8)))


def per_device(pair, token_mask, chain_ids, chain_bias, in_weights, out_weights):
    row_start = lax.axis_index("row") * TOK
    col_start = lax.axis_index("col") * TOK
    valid_rows = lax.dynamic_slice_in_dim(token_mask, row_start, TOK).astype(F32)
    valid_cols = lax.dynamic_slice_in_dim(token_mask, col_start, TOK).astype(F32)
    chain_rows = lax.dynamic_slice_in_dim(chain_ids, row_start, TOK)
    chain_cols = lax.dynamic_slice_in_dim(chain_ids, col_start, TOK)
    mask_out = tile_mask(valid_rows, valid_cols)
    mask_in = tile_mask(valid_cols, valid_rows)
    chain_cols = jnp.broadcast_to(chain_cols[:, None], (TOK, CH))

    tile = ((CH, 16, 128), BF)
    tokens = ((TOK * TOK, CH), F32)
    work = [pltpu.VMEM((TOK * TOK, CH), F32), pltpu.VMEM((PERM, CH), F32), pltpu.VMEM((PERM, CH), F32)]
    product = [pltpu.VMEM((768, 768), BF), pltpu.VMEM((384, 768), BF), pltpu.VMEM((384, 128), F32)]
    dma = pltpu.SemaphoreType.DMA

    first, second, gate, field = call(
        first_kernel,
        [tile, tile, tokens, tokens],
        [pair, chain_rows, chain_cols, chain_bias.reshape(1, CH), in_weights[0], mask_out],
        work,
        "project_out",
        smem=(1,),
    )
    rf, rs = call(
        scatter_out,
        [((2, 8, 16, 16, 128), BF), ((2, 2, 8, 8, 16, 128), BF)],
        [first, second],
        [dma, dma, dma, dma((2,)), dma((2,)), dma((2,))],
        "scatter_out",
        0,
    )
    (made,) = call(triangle_out_kernel, [((8, 16, 16, 128), BF)], [rf, rs], product, "triangle_out")
    (back,) = call(functools.partial(bring_back, False), [tile], [made], [dma, dma], "back_out", 1)
    first, second, gate, field = call(
        middle_kernel,
        [tile, tile, tokens, tokens],
        [field, gate, back, out_weights[0], in_weights[1], mask_in],
        work,
        "project_in",
    )
    rf, rs = call(
        scatter_in,
        [((2, 16, 8, 16, 128), BF), ((16, 8, 16, 128), BF)],
        [first, second],
        [dma, dma, dma, dma, dma, dma],
        "scatter_in",
        2,
    )
    (made,) = call(triangle_in_kernel, [((8, 16, 16, 128), BF)], [rf, rs], product, "triangle_in")
    (back,) = call(functools.partial(bring_back, True), [tile], [made], [dma, dma], "back_in", 3)
    (out,) = call(
        last_kernel,
        [((TOK, TOK, CH), BF)],
        [field, gate, back, out_weights[1]],
        [work[0], work[1]],
        "finish",
    )
    return out


def solution(mesh):
    return jax.shard_map(
        per_device,
        mesh=mesh,
        in_specs=(P("row", "col", None), P(), P(), P(), P(), P()),
        out_specs=P("row", "col", None),
        check_vma=False,
    )
```

time: 466 us -> 136 us (0.29)
  waiting for transfers between devices: 337 us -> 0 us
  Pallas kernels: 0 us -> 133 us
  local copies, waits for them, and re-layouts: 69.5 us -> 2.47 us
  matrix products: 30.1 us -> 0 us
  other arithmetic: 14.4 us -> 0.87 us
  between operations: 13.3 us -> 0.11 us
    reduce_scatter x2 -> x0, waiting for transfers between devices: 198 us -> none  [the longest x1 111 us: per_device(): lax.psum_scatter(jnp.einsum('kic,kjc->ijc', block, second, preferred_elem...]
    all_gather x2 -> x0, waiting for transfers between devices: 139 us -> none  [the longest x1 93.4 us: per_device(): second_rows = lax.all_gather(second, 'row', axis=0, tiled=True)]
    pallas_call x0 -> x9, Pallas kernels: none -> 133 us  [call(): pl.pallas_call(kernel, out_shape=outs, in_specs=[pl.BlockSpec(memory_spac...]
    all_gather x2 -> x0, local copies, waits for them, and re-layouts: 39.4 us -> none  [the longest x1 28.6 us: per_device(): second_rows = lax.all_gather(second, 'row', axis=0, tiled=True)]
    dot_general x6 -> x0, matrix products: 30.1 us -> none  [the longest x1 14.3 us: per_device(): jnp.einsum('jkc,ikc->jic', block, first, preferred_element_type=jnp.float32)]
    convert_element_type x4 -> x0, local copies, waits for them, and re-layouts: 25.8 us -> none  [the longest x1 11.6 us: per_device(): jnp.einsum('jkc,ikc->jic', block, first, preferred_element_type=jnp.float32)]
    reduce_sum x7 -> x0, other arithmetic: 9.39 us -> none  [the longest x4 5.3 us: layer_norm(): spread = jnp.mean(center * center, axis=-1, keepdims=True)]
  transfers between devices with their start and end apart: 4 -> 0, of which waited for: 4 -> 0; matrix products, arithmetic and copies ran while one was open for 1% -> 0% of each run, Pallas kernels for 0% -> 0%
where the time goes in v1:
time: 136 us
  Pallas kernels  133 us (98%)
  local copies, waits for them, and re-layouts  2.47 us (2%)
    pallas_call x9, Pallas kernels, call(): pl.pallas_call(kernel, out_shape=outs, in_specs=[pl.BlockSpec(memory_spac...  133 us

profile of v1, /device:TPU:1, one launch (start us, length us, event | category | flops | bytes accessed | tf_op | source)
XLA Modules:
  0.0 136.0 jit_solution(16492097094288509667)
XLA Ops:
  0.0 0.9 dynamic-slice_convert_fusion
  0.9 0.1 mul.57
  1.0 0.1 reshape.21
  1.1 0.1 mul.51
  1.1 0.1 reshape.22
  1.2 0.1 copy.10
  1.3 0.1 copy.9
  1.4 0.1 broadcast_in_dim.2.cols_ref
  1.5 0.1 mul.48
  1.5 0.1 mul.49
  1.6 0.1 mul.54
  1.7 0.1 mul.55
  1.8 0.8 slice_bitcast_fusion.2
  2.7 0.1 copy-done
  2.9 0.5 copy-done.1
  3.4 2.5 %project_out.1 = (bf16[128,16,128]{2,1,0:T(8,128)(2,1)S(1)}, bf16[128,16,128]{2,1,0:T(8,128)(2,1)S(1)}, f32[1600,128]{1,0:T(8,128)S(1)}, f32[1600,128]{1,0:T(8,128)S(1)}) custom-call(bf16[40,40,128]{2,1,0:T(8,128)(2,1)S(1)} %copy-done, s32[40]{0:T(128)S(1)} %get-tuple-element.37.rows_ref, s32[40,128]{1,0:T(8,128)S(1)} %broadcast_in_dim.2.cols_ref, ...), custom_call_target="tpu_custom_call" | custom-call | tf_op jit(solution)/shard_map/project_out/pallas_call | solution.py:294
  5.9 41.5 %scatter_out.1 = (bf16[2,8,16,16,128]{4,3,2,1,0:T(8,128)(2,1)S(1)}, bf16[2,2,8,8,16,128]{5,4,3,2,1,0:T(8,128)(2,1)S(1)}) custom-call(bf16[128,16,128]{2,1,0:T(8,128)(2,1)S(1)} %get-tuple-element.19.f_ref, bf16[128,16,128]{2,1,0:T(8,128)(2,1)S(1)} %get-tuple-element.20.s_ref), custom_call_target="tpu_custom_call" | custom-call | tf_op jit(solution)/shard_map/scatter_out/pallas_call | solution.py:294
  47.4 1.8 %triangle_out.1.o_ref = bf16[8,16,16,128]{3,2,1,0:T(8,128)(2,1)S(1)} custom-call(bf16[2,8,16,16,128]{4,3,2,1,0:T(8,128)(2,1)S(1)} %get-tuple-element.21.rf, bf16[2,2,8,8,16,128]{5,4,3,2,1,0:T(8,128)(2,1)S(1)} %get-tuple-element.22.rs), custom_call_target="tpu_custom_call" | custom-call | tf_op jit(solution)/shard_map/triangle_out/pallas_call | solution.py:294
  49.2 22.5 %back_out.1.r_ref = bf16[128,16,128]{2,1,0:T(8,128)(2,1)S(1)} custom-call(bf16[8,16,16,128]{3,2,1,0:T(8,128)(2,1)S(1)} %triangle_out.1.o_ref), custom_call_target="tpu_custom_call" | custom-call | tf_op jit(solution)/shard_map/back_out/pallas_call | solution.py:294
  71.7 2.7 %project_in.1 = (bf16[128,16,128]{2,1,0:T(8,128)(2,1)S(1)}, bf16[128,16,128]{2,1,0:T(8,128)(2,1)S(1)}, f32[1600,128]{1,0:T(8,128)S(1)}, f32[1600,128]{1,0:T(8,128)S(1)}) custom-call(f32[1600,128]{1,0:T(8,128)S(1)} %get-tuple-element.17.field_ref, f32[1600,128]{1,0:T(8,128)S(1)} %get-tuple-element.18.gate_ref, bf16[128,16,128]{2,1,0:T(8,128)(2,1)S(1)} %back_out.1.r_ref, ...), custom_call_target="tpu_custom_call" | custom-call | tf_op jit(solution)/shard_map/project_in/pallas_call | solution.py:294
  74.4 34.5 %scatter_in.1 = (bf16[2,16,8,16,128]{4,3,2,1,0:T(8,128)(2,1)S(1)}, bf16[16,8,16,128]{3,2,1,0:T(8,128)(2,1)S(1)}) custom-call(bf16[128,16,128]{2,1,0:T(8,128)(2,1)S(1)} %get-tuple-element.25.f_ref, bf16[128,16,128]{2,1,0:T(8,128)(2,1)S(1)} %get-tuple-element.26.s_ref), custom_call_target="tpu_custom_call" | custom-call | tf_op jit(solution)/shard_map/scatter_in/pallas_call | solution.py:294
  108.9 1.8 %triangle_in.1.o_ref = bf16[8,16,16,128]{3,2,1,0:T(8,128)(2,1)S(1)} custom-call(bf16[2,16,8,16,128]{4,3,2,1,0:T(8,128)(2,1)S(1)} %get-tuple-element.27.rf, bf16[16,8,16,128]{3,2,1,0:T(8,128)(2,1)S(1)} %get-tuple-element.28.rs), custom_call_target="tpu_custom_call" | custom-call | tf_op jit(solution)/shard_map/triangle_in/pallas_call | solution.py:294
  110.7 23.6 %back_in.1.r_ref = bf16[128,16,128]{2,1,0:T(8,128)(2,1)S(1)} custom-call(bf16[8,16,16,128]{3,2,1,0:T(8,128)(2,1)S(1)} %triangle_in.1.o_ref), custom_call_target="tpu_custom_call" | custom-call | tf_op jit(solution)/shard_map/back_in/pallas_call | solution.py:294
  134.3 1.7 %finish.1 = bf16[40,40,128]{2,1,0:T(8,128)(2,1)} custom-call(f32[1600,128]{1,0:T(8,128)S(1)} %get-tuple-element.23.field_ref, f32[1600,128]{1,0:T(8,128)S(1)} %get-tuple-element.24.gate_ref, bf16[128,16,128]{2,1,0:T(8,128)(2,1)S(1)} %back_in.1.r_ref, bf16[128,128]{1,0:T(8,128)(2,1)S(1)} %get-tuple-element.31.wo_ref), custom_call_target="tpu_custom_call" | custom-call | tf_op jit(solution)/shard_map/finish/pallas_call | solution.py:294
  (13 shorter events, 0.1 us)
Async XLA Ops:
  0.0 2.7 %copy-start.2 = (bf16[2,128,640]{2,1,0:T(8,128)(2,1)S(1)}, bf16[2,128,640]{2,1,0:T(8,128)(2,1)}, u32[]{:S(2)}) copy-start(bf16[2,128,640]{2,1,0:T(8,128)(2,1)} %param.10) | copy-start | bytes 983044
  1.8 1.0 copy-start
  2.7 0.7 copy-start.1

commit v2 on v1

v2 whole, which is shorter than its diff:
```python
import jax
import jax.numpy as jnp
from jax import lax
from jax.experimental import pallas as pl
from jax.experimental.pallas import tpu as pltpu
from jax.sharding import PartitionSpec as P


MESH = pl.DeviceIdType.MESH
TOK = 40
ROWS = 16
PLANE = 8
CHIPS = ROWS * PLANE
CH = 128
PERM = 16 * 128
BF = jnp.bfloat16
F32 = jnp.float32
VMEM_LIMIT = 40 * 2**20


def sigmoid(x):
    return 0.5 * jnp.tanh(0.5 * x) + 0.5


def norm_lanes(x):
    center = x - jnp.mean(x, axis=-1, keepdims=True)
    spread = jnp.mean(center * center, axis=-1, keepdims=True)
    return center * lax.rsqrt(spread + 1e-05)


def start_field(pair_ref, chain_rows_ref, chain_cols_ref, bias_ref, field_ref):
    bias = bias_ref[...]
    cols = chain_cols_ref[...]
    for i in range(TOK):
        same = cols == chain_rows_ref[i]
        field_ref[pl.ds(i * TOK, TOK)] = pair_ref[i].astype(F32) + jnp.where(same, bias, 0.0)


def arrange(field_ref, nat, perm, swap):
    nat[...] = norm_lanes(field_ref[...])
    for g in range(16):
        for q in range(3):
            a = 16 * q + g
            at = pl.ds(g * 128 + TOK * q, TOK)
            if a >= TOK:
                perm[at] = jnp.zeros((TOK, CH), F32)
            elif swap:
                perm[at] = nat[pl.ds(a, TOK, stride=TOK)]
            else:
                perm[at] = nat[pl.ds(a * TOK, TOK)]
        perm[pl.ds(g * 128 + 120, 8)] = jnp.zeros((8, CH), F32)


def project(perm, w, mask, out, tiles):
    weights_t = jnp.transpose(w.astype(F32)).astype(BF)
    for part in range(4):
        normed = perm[pl.ds(part * 512, 512)].astype(BF)
        both = lax.dot_general(weights_t, normed, (((1,), (1,)), ((), ())), preferred_element_type=F32)
        value = sigmoid(both[:CH]) * both[CH:]
        for n in range(4):
            g = part * 4 + n
            tiles[pl.ds(g, CH, stride=16)] = value[:, n * 128 : n * 128 + 128] * mask[g : g + 1, :]
    out[...] = tiles[...].reshape(CH, 16, 128).astype(BF)


def project_gate(perm, w, gate_ref, swap):
    for part in range(4):
        normed = perm[pl.ds(part * 512, 512)].astype(BF)
        value = sigmoid(jnp.dot(normed, w, preferred_element_type=F32))
        for n in range(4):
            for q in range(3):
                a = 16 * q + part * 4 + n
                if a < TOK:
                    piece = value[n * 128 + q * TOK : n * 128 + q * TOK + TOK]
                    if swap:
                        gate_ref[pl.ds(a, TOK, stride=TOK)] = piece
                    else:
                        gate_ref[pl.ds(a * TOK, TOK)] = piece


def finish(field_ref, gate_ref, r_ref, weights, tiles):
    x = r_ref[...].astype(F32)
    center = x - jnp.mean(x, axis=0, keepdims=True)
    spread = jnp.mean(center * center, axis=0, keepdims=True)
    tiles[...] = (center * lax.rsqrt(spread + 1e-05)).reshape(CH * 16, 128)
    for g in range(16):
        normed = tiles[pl.ds(g, CH, stride=16)].astype(BF)
        out = lax.dot_general(normed, weights, (((0,), (0,)), ((), ())), preferred_element_type=F32)
        for q in range(3):
            a = 16 * q + g
            if a < TOK:
                at = pl.ds(a * TOK, TOK)
                field_ref[at] = field_ref[at] + gate_ref[at] * out[q * TOK : q * TOK + TOK]


def lanes_between(lo, hi, rows):
    lane = lax.broadcasted_iota(jnp.int32, (rows, 128), 1)
    return (lane >= lo) & (lane < hi)


def roll(x, amount):
    amount = amount % 128
    return pltpu.roll(x, amount, 1) if amount else x


def spread_lanes(blocks, q, rows):
    total = jnp.zeros((rows, 128), F32)
    for m, block in enumerate(blocks):
        total = jnp.where(lanes_between(TOK * m, TOK * m + TOK, rows), roll(block, TOK * (m - q)), total)
    return total


def triangle(load_m, load_n, out_ref, left, right, part):
    part[...] = jnp.zeros((384, 128), F32)
    for group in range(6):
        blocks = range(3 * group, min(3 * group + 3, 16))
        lane = pl.ds(group * 128, 128)
        m_blocks = [load_m(k).astype(F32) for k in blocks]
        n_blocks = [load_n(k).astype(F32) for k in blocks]
        for q in range(3):
            left[pl.ds(q * 256, 256), lane] = spread_lanes(m_blocks, q, 256).astype(BF)
            value = spread_lanes(n_blocks, q, 128)
            for n in range(8):
                depth = 16 if q < 2 else 8
                part[pl.ds(128 * (n // 3) + TOK * (n % 3) + 16 * q, depth)] = value[n * 16 : n * 16 + depth]
        right[:, lane] = part[...].astype(BF)
    for n3 in range(3):
        total = lax.dot_general(
            left[...], right[pl.ds(n3 * 128, 128)], (((1,), (1,)), ((), ())), preferred_element_type=F32
        )
        for m in range(3 if n3 < 2 else 2):
            value = jnp.zeros((256, 128), F32)
            for q in range(3):
                value = jnp.where(
                    lanes_between(TOK * q, TOK * q + TOK, 256),
                    roll(total[q * 256 : q * 256 + 256], TOK * (q - m)),
                    value,
                )
            out_ref[3 * n3 + m] = value.reshape(16, 16, 128).astype(BF)


def place():
    row, col = lax.axis_index("row"), lax.axis_index("col")
    return row, col // 2, col % 2


def each_chip(visit):
    row, chip, core = place()
    rows = [row] + [(row + step) % ROWS for step in range(1, ROWS)]
    for to_row in rows[1:]:
        visit(to_row, chip)

    def column(step, carry):
        to_chip = (chip + step) % PLANE
        for to_row in rows:
            visit(to_row, to_chip)
        return carry

    lax.fori_loop(1, PLANE, column, 0)


def greet():
    row, chip, core = place()
    barrier = pltpu.get_barrier_semaphore()

    def signal(to_row, to_chip):
        pl.semaphore_signal(barrier, inc=1, device_id=(to_row, to_chip * 2 + core), device_id_type=MESH)

    each_chip(signal)
    pl.semaphore_signal(barrier, inc=1, device_id=(row, chip * 2 + 1 - core), device_id_type=MESH)


def send_all(src, dst, send_sem, recv_sem):
    row, chip, core = place()

    def send(to_row, to_chip):
        pltpu.make_async_remote_copy(
            src_ref=src(to_row, to_chip),
            dst_ref=dst,
            send_sem=send_sem,
            recv_sem=recv_sem,
            device_id=(to_row, to_chip * 2 + core),
            device_id_type=MESH,
        ).start()

    each_chip(send)
    pltpu.make_async_copy(src(row, chip), dst, recv_sem).start()


def wait_bytes(ref, sem):
    pltpu.make_async_copy(ref, ref, sem).wait()


def to_sibling(ref, send_sem, recv_sem):
    row, chip, core = place()
    copy = pltpu.make_async_remote_copy(
        src_ref=ref,
        dst_ref=ref,
        send_sem=send_sem,
        recv_sem=recv_sem,
        device_id=(row, chip * 2 + 1 - core),
        device_id_type=MESH,
    )
    copy.start()
    return copy


def kernel(
    pair_ref, rows_ref, cols_ref, bias_ref, w_ref, wo_ref, mask_ref, out_ref,
    field, gate, nat, perm, tiles, f_ref, s_ref, o_ref, rf_out, rs_out, rf_in, rs_in, back_out, back_in,
    left, right, part, send_sem, recv_sem, on_send, on_recv,
):
    row, chip, core = place()
    index = row * PLANE + chip
    some = f_ref.at[pl.ds(0, CHIPS - 1)]
    greet()

    start_field(pair_ref, rows_ref, cols_ref, bias_ref, field)
    arrange(field, nat, perm, False)
    project(perm, w_ref[0, :, :256], mask_ref[0], f_ref, tiles)
    pl.semaphore_wait(pltpu.get_barrier_semaphore(), CHIPS)
    send_all(lambda r, c: f_ref.at[r * PLANE + c], rf_out.at[core, chip, row], send_sem.at[0], recv_sem.at[0])
    project(perm, w_ref[0, :, 256:512], mask_ref[0], s_ref, tiles)
    send_all(
        lambda r, c: s_ref.at[r * PLANE + c],
        rs_out.at[row % 2, core, chip, row // 2],
        send_sem.at[1],
        recv_sem.at[1 + row % 2],
    )
    project_gate(perm, w_ref[0, :, 512:], gate, False)
    wait_bytes(rf_out.at[0], recv_sem.at[0])
    copy_f = to_sibling(rf_out.at[core], on_send.at[0], on_recv.at[0])
    wait_bytes(rs_out.at[0, 0], recv_sem.at[2 - core])
    copy_s = to_sibling(rs_out.at[1 - core, core], on_send.at[1], on_recv.at[1])
    wait_bytes(rs_out.at[0, 0], recv_sem.at[1 + core])
    copy_f.wait()
    copy_s.wait()
    wait_bytes(some, send_sem.at[0])
    wait_bytes(some, send_sem.at[1])
    triangle(
        lambda k: rf_out[k % 2, k // 2].reshape(256, 128),
        lambda k: rs_out[core, k % 2, k // 2].reshape(128, 128),
        o_ref,
        left,
        right,
        part,
    )
    send_all(lambda r, c: o_ref.at[c, r], back_out.at[index], send_sem.at[2], recv_sem.at[3])
    wait_bytes(back_out, recv_sem.at[3])
    wait_bytes(some, send_sem.at[2])
    finish(field, gate, back_out, wo_ref[0], tiles)

    arrange(field, nat, perm, True)
    project(perm, w_ref[1, :, :256], mask_ref[1], f_ref, tiles)
    send_all(lambda r, c: f_ref.at[r * PLANE + c], rf_in.at[core, row, chip], send_sem.at[3], recv_sem.at[4])
    project(perm, w_ref[1, :, 256:512], mask_ref[1], s_ref, tiles)
    send_all(lambda r, c: s_ref.at[r * PLANE + c], rs_in.at[row, chip], send_sem.at[4], recv_sem.at[5])
    project_gate(perm, w_ref[1, :, 512:], gate, True)
    wait_bytes(rf_in.at[0], recv_sem.at[4])
    copy_f = to_sibling(rf_in.at[core], on_send.at[2], on_recv.at[2])
    wait_bytes(rs_in, recv_sem.at[5])
    copy_f.wait()
    wait_bytes(some, send_sem.at[3])
    wait_bytes(some, send_sem.at[4])
    triangle(
        lambda k: jnp.concatenate([rf_in[0, k], rf_in[1, k]], axis=0).reshape(256, 128),
        lambda k: rs_in[k].reshape(128, 128),
        o_ref,
        left,
        right,
        part,
    )
    send_all(
        lambda r, c: o_ref.at[c, (r % 2) * PLANE + r // 2], back_in.at[index], send_sem.at[5], recv_sem.at[6]
    )
    wait_bytes(back_in, recv_sem.at[6])
    wait_bytes(some, send_sem.at[5])
    finish(field, gate, back_in, wo_ref[1], tiles)
    for i in range(TOK):
        out_ref[i] = field[pl.ds(i * TOK, TOK)].astype(BF)


def tile_mask(a_valid, b_valid):
    a = jnp.pad(a_valid, (0, 8)).reshape(3, 16).T
    return jnp.pad((a[:, :, None] * b_valid[None, None, :]).reshape(16, 120), ((0, 0), (0, 8)))


def per_device(pair, token_mask, chain_ids, chain_bias, in_weights, out_weights):
    row_start = lax.axis_index("row") * TOK
    col_start = lax.axis_index("col") * TOK
    valid_rows = lax.dynamic_slice_in_dim(token_mask, row_start, TOK).astype(F32)
    valid_cols = lax.dynamic_slice_in_dim(token_mask, col_start, TOK).astype(F32)
    chain_rows = lax.dynamic_slice_in_dim(chain_ids, row_start, TOK)
    chain_cols = lax.dynamic_slice_in_dim(chain_ids, col_start, TOK)
    masks = jnp.stack([tile_mask(valid_rows, valid_cols), tile_mask(valid_cols, valid_rows)])
    chain_cols = jnp.broadcast_to(chain_cols[:, None], (TOK, CH))
    vmem = pl.BlockSpec(memory_space=pltpu.VMEM)
    dma = pltpu.SemaphoreType.DMA
    return pl.pallas_call(
        kernel,
        out_shape=jax.ShapeDtypeStruct((TOK, TOK, CH), BF),
        in_specs=[vmem, pl.BlockSpec(memory_space=pltpu.SMEM)] + [vmem] * 5,
        out_specs=vmem,
        scratch_shapes=[
            pltpu.VMEM((TOK * TOK, CH), F32),
            pltpu.VMEM((TOK * TOK, CH), F32),
            pltpu.VMEM((TOK * TOK, CH), F32),
            pltpu.VMEM((PERM, CH), F32),
            pltpu.VMEM((PERM, CH), F32),
            pltpu.VMEM((CH, 16, 128), BF),
            pltpu.VMEM((CH, 16, 128), BF),
            pltpu.VMEM((8, 16, 16, 128), BF),
            pltpu.VMEM((2, 8, 16, 16, 128), BF),
            pltpu.VMEM((2, 2, 8, 8, 16, 128), BF),
            pltpu.VMEM((2, 16, 8, 16, 128), BF),
            pltpu.VMEM((16, 8, 16, 128), BF),
            pltpu.VMEM((CH, 16, 128), BF),
            pltpu.VMEM((CH, 16, 128), BF),
            pltpu.VMEM((768, 768), BF),
            pltpu.VMEM((384, 768), BF),
            pltpu.VMEM((384, 128), F32),
            dma((6,)),
            dma((7,)),
            dma((3,)),
            dma((3,)),
        ],
        compiler_params=pltpu.CompilerParams(
            collective_id=0, has_side_effects=True, vmem_limit_bytes=VMEM_LIMIT
        ),
        cost_estimate=pl.CostEstimate(flops=10**9, bytes_accessed=2 * 10**6, transcendentals=10**6),
        name="pairformer",
    )(pair, chain_rows, chain_cols, chain_bias.reshape(1, CH), in_weights, out_weights, masks)


def solution(mesh):
    return jax.shard_map(
        per_device,
        mesh=mesh,
        in_specs=(P("row", "col", None), P(), P(), P(), P(), P()),
        out_specs=P("row", "col", None),
        check_vma=False,
    )
```

time: 136 us -> 110 us (0.81)
  Pallas kernels: 133 us -> 105 us
  local copies, waits for them, and re-layouts: 2.47 us -> 4.16 us
    pallas_call x9 -> x1, Pallas kernels: 133 us -> 105 us  [per_device(): pl.pallas_call(kernel, out_shape=jax.ShapeDtypeStruct((TOK, TOK, CH), BF)...]
    unnamed x6 -> x9, local copies, waits for them, and re-layouts: 0.69 us -> 3.23 us
where the time goes in v2:
time: 110 us
  Pallas kernels  105 us (95%)
  local copies, waits for them, and re-layouts  4.16 us (4%)
    pallas_call x1, Pallas kernels, per_device(): pl.pallas_call(kernel, out_shape=jax.ShapeDtypeStruct((TOK, TOK, CH), BF)...  105 us
    unnamed x9, local copies, waits for them, and re-layouts  3.23 us

profile of v2, /device:TPU:1, one launch (start us, length us, event | category | flops | bytes accessed | tf_op | source)
XLA Modules:
  0.0 109.9 jit_solution(5154791569904157924)
XLA Ops:
  0.0 0.0 copy-start.1
  0.0 0.9 dynamic-slice_convert_fusion.1
  0.9 0.1 mul.51
  1.0 0.1 reshape.22
  1.1 0.1 mul.57
  1.1 0.1 reshape.21
  1.2 0.1 copy.9
  1.3 0.1 copy.10
  1.4 0.1 broadcast_in_dim.2.cols_ref
  1.5 0.1 mul.54
  1.5 0.1 mul.55
  1.6 0.1 mul.48
  1.7 0.1 mul.49
  1.8 0.0 copy-start.3
  1.8 0.0 copy-done.1
  1.9 0.6 copy-done.3
  2.5 0.0 copy-start
  2.5 1.0 copy-done
  3.5 0.0 copy-start.2
  3.5 0.8 copy-done.2
  4.3 104.8 %pairformer.1 = bf16[40,40,128]{2,1,0:T(8,128)(2,1)S(1)} custom-call(bf16[40,40,128]{2,1,0:T(8,128)(2,1)S(1)} %copy-done, s32[40]{0:T(128)S(1)} %get-tuple-element.9.rows_ref, s32[40,128]{1,0:T(8,128)S(1)} %broadcast_in_dim.2.cols_ref, f32[1,128]{1,0:T(1,128)S(1)} %bitcast.7, bf16[2,128,640]{2,1,0:T(8,128)(2,1)S(1)} %copy-done.1, ...), custom_call_target="tpu_custom_call" | custom-call | flops 1000000000 | bytes 2000000 | tf_op jit(solution)/shard_map/pairformer/pallas_call | solution.py:299
  109.1 0.8 copy.12
  (9 shorter events, 0.0 us)
Async XLA Ops:
  0.0 1.9 %copy-start.1 = (bf16[2,128,640]{2,1,0:T(8,128)(2,1)S(1)}, bf16[2,128,640]{2,1,0:T(8,128)(2,1)}, u32[]{:S(2)}) copy-start(bf16[2,128,640]{2,1,0:T(8,128)(2,1)} %w_ref.1) | copy-start | bytes 983044
  1.8 0.7 copy-start.3
  2.5 1.0 copy-start
  3.5 0.8 copy-start.2

commit v3 on v2

v3 whole, which is shorter than its diff:
```python
import jax
import jax.numpy as jnp
from jax import lax
from jax.experimental import pallas as pl
from jax.experimental.pallas import tpu as pltpu
from jax.sharding import PartitionSpec as P


MESH = pl.DeviceIdType.MESH
TOK = 40
ROWS = 16
PLANE = 8
CHIPS = ROWS * PLANE
CH = 128
PERM = 16 * 128
BF = jnp.bfloat16
F32 = jnp.float32
VMEM_LIMIT = 60 * 2**20
STEPS_X = (2, 1, 3, 0)
STEPS_Y = (2, 1, 3, 0)
STEPS_Z = (4, 0, 3, 5, 1, 7, 2, 6)


def sigmoid(x):
    return 0.5 * jnp.tanh(0.5 * x) + 0.5


def norm_lanes(x):
    center = x - jnp.mean(x, axis=-1, keepdims=True)
    spread = jnp.mean(center * center, axis=-1, keepdims=True)
    return center * lax.rsqrt(spread + 1e-05)


def start_field(pair_ref, ids_ref, bias_ref, field_ref, column):
    row, col = lax.axis_index("row"), lax.axis_index("col")
    for j in range(TOK):
        column[j : j + 1, :] = jnp.full((1, CH), ids_ref[col * TOK + j], jnp.int32)
    bias = bias_ref[...]
    cols = column[...]
    for i in range(TOK):
        same = cols == ids_ref[row * TOK + i]
        field_ref[pl.ds(i * TOK, TOK)] = pair_ref[i].astype(F32) + jnp.where(same, bias, 0.0)


def tile_masks(valid_ref, mask):
    row, col = lax.axis_index("row"), lax.axis_index("col")
    lane = lax.broadcasted_iota(jnp.int32, (1, 128), 1)
    third = (lane >= TOK).astype(jnp.int32) + (lane >= 2 * TOK).astype(jnp.int32)
    place_b = jnp.where(lane < 3 * TOK, lane - TOK * third, TOK)
    rows = [valid_ref[row * TOK + n].astype(F32) for n in range(TOK)]
    cols = [valid_ref[col * TOK + n].astype(F32) for n in range(TOK)]
    for d, (a_valid, b_valid) in enumerate(((rows, cols), (cols, rows))):
        along = jnp.zeros((1, 128), F32)
        for b in range(TOK):
            along = jnp.where(place_b == b, b_valid[b], along)
        for g in range(16):
            low = jnp.where(third == 0, a_valid[g], a_valid[16 + g])
            high = a_valid[32 + g] if 32 + g < TOK else 0.0
            mask[d, g : g + 1, :] = jnp.where(third == 2, high, low) * along


def arrange(field_ref, nat, perm, swap):
    nat[...] = norm_lanes(field_ref[...])
    for g in range(16):
        for q in range(3):
            a = 16 * q + g
            at = pl.ds(g * 128 + TOK * q, TOK)
            if a >= TOK:
                perm[at] = jnp.zeros((TOK, CH), F32)
            elif swap:
                perm[at] = nat[pl.ds(a, TOK, stride=TOK)]
            else:
                perm[at] = nat[pl.ds(a * TOK, TOK)]
        perm[pl.ds(g * 128 + 120, 8)] = jnp.zeros((8, CH), F32)


def project(perm, w, mask, out, tiles):
    weights_t = jnp.transpose(w.astype(F32)).astype(BF)
    for part in range(4):
        normed = perm[pl.ds(part * 512, 512)].astype(BF)
        both = lax.dot_general(weights_t, normed, (((1,), (1,)), ((), ())), preferred_element_type=F32)
        value = sigmoid(both[:CH]) * both[CH:]
        for n in range(4):
            g = part * 4 + n
            tiles[pl.ds(g, CH, stride=16)] = value[:, n * 128 : n * 128 + 128] * mask[g : g + 1, :]
    out[...] = tiles[...].reshape(CH, 16, 128).astype(BF)


def project_gate(perm, w, gate_ref, swap):
    for part in range(4):
        normed = perm[pl.ds(part * 512, 512)].astype(BF)
        value = sigmoid(jnp.dot(normed, w, preferred_element_type=F32))
        for n in range(4):
            for q in range(3):
                a = 16 * q + part * 4 + n
                if a < TOK:
                    piece = value[n * 128 + q * TOK : n * 128 + q * TOK + TOK]
                    if swap:
                        gate_ref[pl.ds(a, TOK, stride=TOK)] = piece
                    else:
                        gate_ref[pl.ds(a * TOK, TOK)] = piece


def finish(field_ref, gate_ref, r_ref, weights, tiles):
    x = r_ref[...].astype(F32)
    center = x - jnp.mean(x, axis=0, keepdims=True)
    spread = jnp.mean(center * center, axis=0, keepdims=True)
    tiles[...] = (center * lax.rsqrt(spread + 1e-05)).reshape(CH * 16, 128)
    for g in range(16):
        normed = tiles[pl.ds(g, CH, stride=16)].astype(BF)
        out = lax.dot_general(normed, weights, (((0,), (0,)), ((), ())), preferred_element_type=F32)
        for q in range(3):
            a = 16 * q + g
            if a < TOK:
                at = pl.ds(a * TOK, TOK)
                field_ref[at] = field_ref[at] + gate_ref[at] * out[q * TOK : q * TOK + TOK]


def lanes_between(lo, hi, rows):
    lane = lax.broadcasted_iota(jnp.int32, (rows, 128), 1)
    return (lane >= lo) & (lane < hi)


def roll(x, amount):
    amount = amount % 128
    return pltpu.roll(x, amount, 1) if amount else x


def spread_lanes(blocks, q, rows):
    total = jnp.zeros((rows, 128), F32)
    for m, block in enumerate(blocks):
        total = jnp.where(lanes_between(TOK * m, TOK * m + TOK, rows), roll(block, TOK * (m - q)), total)
    return total


def assemble(load_m, load_n, left, right, part):
    part[...] = jnp.zeros((384, 128), F32)
    for group in range(6):
        blocks = range(3 * group, min(3 * group + 3, 16))
        lane = pl.ds(group * 128, 128)
        m_blocks = [load_m(k).astype(F32) for k in blocks]
        n_blocks = [load_n(k).astype(F32) for k in blocks]
        for q in range(3):
            left[pl.ds(q * 256, 256), lane] = spread_lanes(m_blocks, q, 256).astype(BF)
            value = spread_lanes(n_blocks, q, 128)
            for n in range(8):
                depth = 16 if q < 2 else 8
                part[pl.ds(128 * (n // 3) + TOK * (n % 3) + 16 * q, depth)] = value[n * 16 : n * 16 + depth]
        right[:, lane] = part[...].astype(BF)


def multiply(x_to, left, right, out_ref):
    rows = [left[pl.ds(pl.multiple_of(q * 256 + x_to * 64, 64), 64)] for q in range(3)]
    total = lax.dot_general(
        jnp.concatenate(rows, axis=0), right[...], (((1,), (1,)), ((), ())), preferred_element_type=F32
    )
    for n in range(8):
        n3, m = n // 3, n % 3
        value = jnp.zeros((64, 128), F32)
        for q in range(3):
            value = jnp.where(
                lanes_between(TOK * q, TOK * q + TOK, 64),
                roll(total[q * 64 : q * 64 + 64, n3 * 128 : n3 * 128 + 128], TOK * (q - m)),
                value,
            )
        out_ref[n, pl.ds(x_to * 4, 4)] = value.reshape(4, 16, 128).astype(BF)


def place():
    row, col = lax.axis_index("row"), lax.axis_index("col")
    return row, col // 2, col % 2


def greet(line):
    row, chip, core = place()
    barrier = pltpu.get_barrier_semaphore()
    chips = [(chip + step) % PLANE for step in range(1, PLANE)]
    for step in range(1, ROWS):
        pl.semaphore_signal(
            barrier, inc=1, device_id=((row + step) % ROWS, chip * 2 + core), device_id_type=MESH
        )
    for to_chip in chips:
        pl.semaphore_signal(barrier, inc=1, device_id=(row, to_chip * 2 + core), device_id_type=MESH)
    pl.semaphore_signal(barrier, inc=1, device_id=(row, chip * 2 + 1 - core), device_id_type=MESH)

    def arrived():
        pl.semaphore_wait(barrier, ROWS + PLANE - 1)
        for to_chip in chips:
            pl.semaphore_signal(line, inc=1, device_id=(row, to_chip * 2 + core), device_id_type=MESH)

    return arrived


class Offsets:
    def __init__(self):
        self.row, self.chip, self.core = place()
        x, y, z = self.row // 4, self.chip // 2, self.row % 4 * 2 + self.chip % 2
        self.x = [x] + [(x + step) % 4 for step in range(1, 4)]
        y = [y] + [(y + step) % 4 for step in range(1, 4)]
        z = [z] + [(z + step) % 8 for step in range(1, 8)]
        self.y = [value * 2 for value in y]
        self.z = [(value // 2, value % 2) for value in z]

    def at(self, dx, dy, dz):
        return self.x[dx] * 4 + self.z[dz][0], self.y[dy] + self.z[dz][1]

    def send(self, dx, arrays):
        for dy in STEPS_Y:
            for dz in STEPS_Z:
                to_row, to_chip = self.at(dx, dy, dz)
                for src, dst, send_sem, recv_sem in arrays:
                    if (dx, dy, dz) == (0, 0, 0):
                        pltpu.make_async_copy(src(self.row, self.chip), dst, recv_sem).start()
                    else:
                        pltpu.make_async_remote_copy(
                            src_ref=src(to_row, to_chip),
                            dst_ref=dst,
                            send_sem=send_sem,
                            recv_sem=recv_sem,
                            device_id=(to_row, to_chip * 2 + self.core),
                            device_id_type=MESH,
                        ).start()


def wait_bytes(ref, sem):
    pltpu.make_async_copy(ref, ref, sem).wait()


def to_sibling(ref, send_sem, recv_sem):
    row, chip, core = place()
    copy = pltpu.make_async_remote_copy(
        src_ref=ref,
        dst_ref=ref,
        send_sem=send_sem,
        recv_sem=recv_sem,
        device_id=(row, chip * 2 + 1 - core),
        device_id_type=MESH,
    )
    copy.start()
    return copy


def kernel(
    pair_hbm, valid_ref, ids_ref, bias_ref, w_hbm, wo_hbm, out_ref,
    pair_ref, w_ref, wo_ref, mask_ref, column, field, gate, nat, perm, tiles, f_ref, s_ref, o_ref,
    rf_out, rs_out, rf_in, rs_in, back_out, back_in, left, right, part,
    load_sem, line, send_sem, f_recv, s_recv, s_in_recv, back_recv, on_send, on_recv,
):
    row, chip, core = place()
    index = row * PLANE + chip
    some = f_ref.at[pl.ds(0, CHIPS - 1)]
    loads = [
        pltpu.make_async_copy(src, dst, load_sem.at[n])
        for n, (src, dst) in enumerate(((pair_hbm, pair_ref), (w_hbm, w_ref), (wo_hbm, wo_ref)))
    ]
    for load in loads:
        load.start()
    arrived = greet(line)
    offsets = Offsets()

    tile_masks(valid_ref, mask_ref)
    loads[0].wait()
    start_field(pair_ref, ids_ref, bias_ref, field, column)
    arrange(field, nat, perm, False)
    arrived()
    loads[1].wait()
    project(perm, w_ref[0, :, :256], mask_ref[0], f_ref, tiles)
    project(perm, w_ref[0, :, 256:512], mask_ref[0], s_ref, tiles)
    pl.semaphore_wait(line, PLANE - 1)
    parity = row % 2
    for dx in STEPS_X:
        offsets.send(
            dx,
            [
                (lambda r, c: f_ref.at[r * PLANE + c], rf_out.at[core, chip, row], send_sem.at[0], f_recv.at[dx]),
                (
                    lambda r, c: s_ref.at[r * PLANE + c],
                    rs_out.at[parity, core, chip, row // 2],
                    send_sem.at[1],
                    s_recv.at[parity * 4 + dx],
                ),
            ],
        )
    project_gate(perm, w_ref[0, :, 512:], gate, False)
    loads[2].wait()
    copies = []
    for dx in STEPS_X:
        x_from = offsets.x[-dx % 4]
        whole = rf_out.at[core, :, pl.ds(x_from * 4, 4)]
        wait_bytes(whole, f_recv.at[dx])
        copies.append(to_sibling(whole, on_send.at[dx], on_recv.at[dx]))
        half = rs_out.at[1 - core, core, :, pl.ds(x_from * 2, 2)]
        wait_bytes(half, s_recv.at[(1 - core) * 4 + dx])
        copies.append(to_sibling(half, on_send.at[4 + dx], on_recv.at[4 + dx]))
    for dx in STEPS_X:
        wait_bytes(rs_out.at[core, core, :, pl.ds(offsets.x[-dx % 4] * 2, 2)], s_recv.at[core * 4 + dx])
    for copy in copies:
        copy.wait()
    assemble(
        lambda k: rf_out[k % 2, k // 2].reshape(256, 128),
        lambda k: rs_out[core, k % 2, k // 2].reshape(128, 128),
        left,
        right,
        part,
    )
    for dx in STEPS_X:
        multiply(offsets.x[dx], left, right, o_ref)
        offsets.send(dx, [(lambda r, c: o_ref.at[c, r], back_out.at[index], send_sem.at[2], back_recv.at[0])])
    wait_bytes(some, send_sem.at[0])
    wait_bytes(some, send_sem.at[1])
    wait_bytes(back_out, back_recv.at[0])
    wait_bytes(some, send_sem.at[2])
    finish(field, gate, back_out, wo_ref[0], tiles)

    arrange(field, nat, perm, True)
    project(perm, w_ref[1, :, :256], mask_ref[1], f_ref, tiles)
    project(perm, w_ref[1, :, 256:512], mask_ref[1], s_ref, tiles)
    for dx in STEPS_X:
        offsets.send(
            dx,
            [
                (lambda r, c: f_ref.at[r * PLANE + c], rf_in.at[core, row, chip], send_sem.at[3], f_recv.at[4 + dx]),
                (lambda r, c: s_ref.at[r * PLANE + c], rs_in.at[row, chip], send_sem.at[4], s_in_recv),
            ],
        )
    project_gate(perm, w_ref[1, :, 512:], gate, True)
    copies = []
    for dx in STEPS_X:
        whole = rf_in.at[core, pl.ds(offsets.x[-dx % 4] * 4, 4)]
        wait_bytes(whole, f_recv.at[4 + dx])
        copies.append(to_sibling(whole, on_send.at[8 + dx], on_recv.at[8 + dx]))
    wait_bytes(rs_in, s_in_recv)
    for copy in copies:
        copy.wait()
    assemble(
        lambda k: jnp.concatenate([rf_in[n % 2, k, n // 2] for n in range(16)], axis=0),
        lambda k: rs_in[k].reshape(128, 128),
        left,
        right,
        part,
    )
    for dx in STEPS_X:
        multiply(offsets.x[dx], left, right, o_ref)
        offsets.send(dx, [(lambda r, c: o_ref.at[c, r], back_in.at[index], send_sem.at[5], back_recv.at[1])])
    wait_bytes(some, send_sem.at[3])
    wait_bytes(some, send_sem.at[4])
    wait_bytes(back_in, back_recv.at[1])
    wait_bytes(some, send_sem.at[5])
    finish(field, gate, back_in, wo_ref[1], tiles)
    for i in range(TOK):
        out_ref[i] = field[pl.ds(i * TOK, TOK)].astype(BF)


def per_device(pair, token_mask, chain_ids, chain_bias, in_weights, out_weights):
    hbm = pl.BlockSpec(memory_space=pl.ANY)
    smem = pl.BlockSpec(memory_space=pltpu.SMEM)
    vmem = pl.BlockSpec(memory_space=pltpu.VMEM)
    dma = pltpu.SemaphoreType.DMA
    tokens = pltpu.VMEM((TOK * TOK, CH), F32)
    return pl.pallas_call(
        kernel,
        out_shape=jax.ShapeDtypeStruct((TOK, TOK, CH), BF),
        in_specs=[hbm, smem, smem, vmem, hbm, hbm],
        out_specs=vmem,
        scratch_shapes=[
            pltpu.VMEM((TOK, TOK, CH), BF),
            pltpu.VMEM((2, CH, 5 * CH), BF),
            pltpu.VMEM((2, CH, CH), BF),
            pltpu.VMEM((2, 16, 128), F32),
            pltpu.VMEM((TOK, CH), jnp.int32),
            tokens,
            tokens,
            tokens,
            pltpu.VMEM((PERM, CH), F32),
            pltpu.VMEM((PERM, CH), F32),
            pltpu.VMEM((CH, 16, 128), BF),
            pltpu.VMEM((CH, 16, 128), BF),
            pltpu.VMEM((8, 16, 16, 128), BF),
            pltpu.VMEM((2, 8, 16, 16, 128), BF),
            pltpu.VMEM((2, 2, 8, 8, 16, 128), BF),
            pltpu.VMEM((2, 16, 8, 16, 128), BF),
            pltpu.VMEM((16, 8, 16, 128), BF),
            pltpu.VMEM((CH, 16, 128), BF),
            pltpu.VMEM((CH, 16, 128), BF),
            pltpu.VMEM((768, 768), BF),
            pltpu.VMEM((384, 768), BF),
            pltpu.VMEM((384, 128), F32),
            dma((3,)),
            pltpu.SemaphoreType.REGULAR,
            dma((6,)),
            dma((8,)),
            dma((8,)),
            dma,
            dma((2,)),
            dma((12,)),
            dma((12,)),
        ],
        compiler_params=pltpu.CompilerParams(
            collective_id=0, has_side_effects=True, vmem_limit_bytes=VMEM_LIMIT
        ),
        cost_estimate=pl.CostEstimate(flops=10**9, bytes_accessed=2 * 10**6, transcendentals=10**6),
        name="pairformer",
    )(pair, token_mask, chain_ids, chain_bias.reshape(1, CH), in_weights, out_weights)


def solution(mesh):
    return jax.shard_map(
        per_device,
        mesh=mesh,
        in_specs=(P("row", "col", None), P(), P(), P(), P(), P()),
        out_specs=P("row", "col", None),
        check_vma=False,
    )
```

time: 110 us -> 106 us (0.964)
  local copies, waits for them, and re-layouts: 4.16 us -> 1.79 us
    unnamed x9 -> x1, local copies, waits for them, and re-layouts: 3.23 us -> 1.79 us
where the time goes in v3:
time: 106 us; the launch traced here: 105 us
  Pallas kernels  104 us (98%)
  local copies, waits for them, and re-layouts  1.79 us (2%)
    pallas_call x1, Pallas kernels, per_device(): pl.pallas_call(kernel, out_shape=jax.ShapeDtypeStruct((TOK, TOK, CH), BF)...  104 us

profile of v3, /device:TPU:1, one launch (start us, length us, event | category | flops | bytes accessed | tf_op | source)
XLA Modules:
  0.0 105.5 jit_solution(374137131332624286)
XLA Ops:
  0.0 103.7 %pairformer.1 = bf16[40,40,128]{2,1,0:T(8,128)(2,1)} custom-call(bf16[40,40,128]{2,1,0:T(8,128)(2,1)} %pair_hbm.1, s32[640]{0:T(1024)} %valid_ref.1, s32[640]{0:T(1024)} %ids_ref.1, f32[1,128]{1,0:T(1,128)} %bitcast.1, bf16[2,128,640]{2,1,0:T(8,128)(2,1)} %w_hbm.1, bf16[2,128,128]{2,1,0:T(8,128)(2,1)} %wo_hbm.1), custom_call_target="tpu_custom_call" | custom-call | flops 1000000000 | bytes 2000000 | tf_op jit(solution)/shard_map/pairformer/pallas_call | solution.py:360
  103.7 1.8 %copy.8 = bf16[40,40,128]{2,1,0:T(8,128)(2,1)} copy(bf16[40,40,128]{2,1,0:T(8,128)(2,1)} %pairformer.1) | data formatting | bytes 819200

commit v4 on v3

v4 whole, which is shorter than its diff:
```python
import jax
import jax.numpy as jnp
from jax import lax
from jax.experimental import pallas as pl
from jax.experimental.pallas import tpu as pltpu
from jax.sharding import PartitionSpec as P


MESH = pl.DeviceIdType.MESH
TOK = 40
ROWS = 16
PLANE = 8
CHIPS = ROWS * PLANE
CH = 128
PERM = 16 * 128
BF = jnp.bfloat16
F32 = jnp.float32
VMEM_LIMIT = 60 * 2**20
STEPS_Y = (2, 1, 3, 0)
STEPS_Z = (4, 0, 3, 5, 1, 7, 2, 6)
GROUPS = ((0, 1, 2), (3, 4, 5), (6, 7), (8, 9, 10), (11, 12, 13), (14, 15))


def sigmoid(x):
    return 0.5 * jnp.tanh(0.5 * x) + 0.5


def norm_lanes(x):
    center = x - jnp.mean(x, axis=-1, keepdims=True)
    spread = jnp.mean(center * center, axis=-1, keepdims=True)
    return center * lax.rsqrt(spread + 1e-05)


def start_field(pair_ref, ids_ref, bias_ref, field_ref, column):
    row, col = lax.axis_index("row"), lax.axis_index("col")
    for j in range(TOK):
        column[j : j + 1, :] = jnp.full((1, CH), ids_ref[col * TOK + j], jnp.int32)
    bias = bias_ref[...]
    cols = column[...]
    for i in range(TOK):
        same = cols == ids_ref[row * TOK + i]
        field_ref[pl.ds(i * TOK, TOK)] = pair_ref[i].astype(F32) + jnp.where(same, bias, 0.0)


def tile_masks(valid_ref, mask):
    row, col = lax.axis_index("row"), lax.axis_index("col")
    lane = lax.broadcasted_iota(jnp.int32, (1, 128), 1)
    third = (lane >= TOK).astype(jnp.int32) + (lane >= 2 * TOK).astype(jnp.int32)
    place_b = jnp.where(lane < 3 * TOK, lane - TOK * third, TOK)
    rows = [valid_ref[row * TOK + n].astype(F32) for n in range(TOK)]
    cols = [valid_ref[col * TOK + n].astype(F32) for n in range(TOK)]
    for d, (a_valid, b_valid) in enumerate(((rows, cols), (cols, rows))):
        along = jnp.zeros((1, 128), F32)
        for b in range(TOK):
            along = jnp.where(place_b == b, b_valid[b], along)
        for g in range(16):
            low = jnp.where(third == 0, a_valid[g], a_valid[16 + g])
            high = a_valid[32 + g] if 32 + g < TOK else 0.0
            mask[d, g : g + 1, :] = jnp.where(third == 2, high, low) * along


def arrange(field_ref, nat, perm, swap):
    nat[...] = norm_lanes(field_ref[...])
    for g in range(16):
        for q in range(3):
            a = 16 * q + g
            at = pl.ds(g * 128 + TOK * q, TOK)
            if a >= TOK:
                perm[at] = jnp.zeros((TOK, CH), F32)
            elif swap:
                perm[at] = nat[pl.ds(a, TOK, stride=TOK)]
            else:
                perm[at] = nat[pl.ds(a * TOK, TOK)]
        perm[pl.ds(g * 128 + 120, 8)] = jnp.zeros((8, CH), F32)


def project(perm, w, mask, tiles):
    weights_t = jnp.transpose(w.astype(F32)).astype(BF)
    for part in range(4):
        normed = perm[pl.ds(part * 512, 512)].astype(BF)
        both = lax.dot_general(weights_t, normed, (((1,), (1,)), ((), ())), preferred_element_type=F32)
        value = sigmoid(both[:CH]) * both[CH:]
        for n in range(4):
            g = part * 4 + n
            tiles[pl.ds(g, CH, stride=16)] = value[:, n * 128 : n * 128 + 128] * mask[g : g + 1, :]
    return tiles[...].reshape(CH, 2, 8, 128).astype(BF)


def project_gate(perm, w, gate_ref, swap):
    for part in range(4):
        normed = perm[pl.ds(part * 512, 512)].astype(BF)
        value = sigmoid(jnp.dot(normed, w, preferred_element_type=F32))
        for n in range(4):
            for q in range(3):
                a = 16 * q + part * 4 + n
                if a < TOK:
                    piece = value[n * 128 + q * TOK : n * 128 + q * TOK + TOK]
                    if swap:
                        gate_ref[pl.ds(a, TOK, stride=TOK)] = piece
                    else:
                        gate_ref[pl.ds(a * TOK, TOK)] = piece


def finish(field_ref, gate_ref, r_ref, weights, tiles, half):
    x = r_ref[...].astype(F32)
    center = x - jnp.mean(x, axis=0, keepdims=True)
    spread = jnp.mean(center * center, axis=0, keepdims=True)
    tiles[pl.ds(0, CH * 8)] = (center * lax.rsqrt(spread + 1e-05)).reshape(CH * 8, 128)
    for g in range(8):
        normed = tiles[pl.ds(g, CH, stride=8)].astype(BF)
        out = lax.dot_general(normed, weights, (((0,), (0,)), ((), ())), preferred_element_type=F32)
        for q in range(3 - half):
            a = 16 * q + 8 * half + g
            at = pl.ds(a * TOK, TOK)
            field_ref[at] = field_ref[at] + gate_ref[at] * out[q * TOK : q * TOK + TOK]


def lanes_between(lo, hi, rows):
    lane = lax.broadcasted_iota(jnp.int32, (rows, 128), 1)
    return (lane >= lo) & (lane < hi)


def roll(x, amount):
    amount = amount % 128
    return pltpu.roll(x, amount, 1) if amount else x


def spread_lanes(blocks, q, rows):
    total = jnp.zeros((rows, 128), F32)
    for m, block in enumerate(blocks):
        total = jnp.where(lanes_between(TOK * m, TOK * m + TOK, rows), roll(block, TOK * (m - q)), total)
    return total


def assemble_right(load_n, right, part):
    part[...] = jnp.zeros((768, 128), F32)
    for group, blocks in enumerate(GROUPS):
        parts = [load_n(k).astype(F32).reshape(256, 128) for k in blocks]
        for q in range(3):
            value = spread_lanes(parts, q, 256)
            for n in range(16):
                depth = 16 if q < 2 else 8
                part[pl.ds(128 * (n // 3) + TOK * (n % 3) + 16 * q, depth)] = value[n * 16 : n * 16 + depth]
        right[:, pl.ds(group * 128, 128)] = part[...].astype(BF)


def multiply(load_m, half, left, right, out_ref):
    for group, blocks in enumerate(GROUPS):
        parts = [load_m(k).astype(F32).reshape(64, 128) for k in blocks]
        for q in range(3 - half):
            left[pl.ds(q * 64, 64), pl.ds(group * 128, 128)] = spread_lanes(parts, q, 64).astype(BF)
    rows = left[pl.ds(0, 64 * (3 - half))]
    total = lax.dot_general(rows, right[...], (((1,), (1,)), ((), ())), preferred_element_type=F32)
    for n in range(16):
        n3, m = n // 3, n % 3
        value = jnp.zeros((64, 128), F32)
        for q in range(3 - half):
            value = jnp.where(
                lanes_between(TOK * q, TOK * q + TOK, 64),
                roll(total[q * 64 : q * 64 + 64, n3 * 128 : n3 * 128 + 128], TOK * (q - m)),
                value,
            )
        out_ref[n] = value.reshape(8, 8, 128).astype(BF)


def place():
    row, col = lax.axis_index("row"), lax.axis_index("col")
    return row, col // 2, col % 2


def greet(line):
    row, chip, core = place()
    barrier = pltpu.get_barrier_semaphore()
    chips = [(chip + step) % PLANE for step in range(1, PLANE)]
    for step in range(1, ROWS):
        for other in (core, 1 - core):
            pl.semaphore_signal(
                barrier, inc=1, device_id=((row + step) % ROWS, chip * 2 + other), device_id_type=MESH
            )
    for to_chip in chips:
        pl.semaphore_signal(barrier, inc=1, device_id=(row, to_chip * 2 + core), device_id_type=MESH)
    pl.semaphore_signal(barrier, inc=1, device_id=(row, chip * 2 + 1 - core), device_id_type=MESH)

    def arrived():
        pl.semaphore_wait(barrier, 2 * (ROWS - 1) + PLANE)
        for to_chip in chips:
            pl.semaphore_signal(line, inc=1, device_id=(row, to_chip * 2 + core), device_id_type=MESH)

    return arrived


def remote(src, dst, send_sem, recv_sem, to_row, to_col):
    return pltpu.make_async_remote_copy(
        src_ref=src,
        dst_ref=dst,
        send_sem=send_sem,
        recv_sem=recv_sem,
        device_id=(to_row, to_col),
        device_id_type=MESH,
    )


class Sends:
    def __init__(self):
        self.row, self.chip, self.core = place()
        self.x, y, z_hi, z_lo = self.row // 4, self.chip // 2, self.row % 4, self.chip % 2
        z = [z_hi * 2 + z_lo] + [(z_hi * 2 + z_lo + step) % 8 for step in range(1, 8)]
        self.y = [y * 2] + [(y + step) % 4 * 2 for step in range(1, 4)]
        self.z = [(value // 2, value % 2) for value in z]
        self.z_own = [
            (self.core + 2 * ((z_hi // 2 + s) % 2), (z_lo + t) % 2) for s, t in ((1, 0), (0, 0), (1, 1), (0, 1))
        ]

    def every(self, visit):
        def along(step, carry):
            for dy in STEPS_Y:
                visit((self.x + step) % 4, dy, False)
            return carry

        lax.fori_loop(1, 4, along, 0)
        for dy in STEPS_Y:
            visit(self.x, dy, dy == 0)

    def to_chips(self, src, dst, send_sem, recv_sem, to_core):
        def visit(x, dy, line):
            for dz in STEPS_Z:
                to_row, to_chip = x * 4 + self.z[dz][0], self.y[dy] + self.z[dz][1]
                if not (line and dz == 0):
                    remote(
                        src(to_row * PLANE + to_chip), dst, send_sem, recv_sem, to_row, to_chip * 2 + to_core
                    ).start()

        self.every(visit)
        self.own(src(self.row * PLANE + self.chip), dst, send_sem, recv_sem, self.row, self.chip * 2 + to_core, to_core)

    def own(self, src, dst, send_sem, recv_sem, to_row, to_col, to_core):
        if to_core is self.core:
            pltpu.make_async_copy(src, dst, recv_sem).start()
            return

        @pl.when(to_core == self.core)
        def _():
            pltpu.make_async_copy(src, dst, recv_sem).start()

        @pl.when(to_core != self.core)
        def _():
            remote(src, dst, send_sem, recv_sem, to_row, to_col).start()

    def to_owners(self, o_ref, dst, send_sem, recv_sem):
        parity = self.row % 2

        def visit(x, dy, line):
            for n, (z_hi, z_lo) in enumerate(self.z_own):
                to_row, to_chip = x * 4 + z_hi, self.y[dy] + z_lo
                for other in (0, 1):
                    to_col = to_chip * 2 + (1 - self.core if other else self.core)
                    src = o_ref.at[to_col, to_row // 2]
                    copy = remote(src, dst, send_sem, recv_sem, to_row, to_col)
                    if line and n == 1 and not other:

                        @pl.when(parity == self.core)
                        def _():
                            pltpu.make_async_copy(src, dst, recv_sem).start()

                        @pl.when(parity != self.core)
                        def _():
                            copy.start()

                    else:
                        copy.start()

        self.every(visit)

    def sent(self, ref, send_sem, across):
        wait_bytes(ref.at[pl.ds(0, CHIPS - 1)], send_sem)
        if across:

            @pl.when(self.row % 2 != self.core)
            def _():
                wait_bytes(ref.at[0], send_sem)


def wait_bytes(ref, sem):
    pltpu.make_async_copy(ref, ref, sem).wait()


def to_sibling(ref, send_sem, recv_sem):
    row, chip, core = place()
    copy = remote(ref, ref, send_sem, recv_sem, row, chip * 2 + 1 - core)
    copy.start()
    return copy


def kernel(
    pair_hbm, valid_ref, ids_ref, bias_ref, w_hbm, wo_hbm, out_ref,
    pair_ref, w_ref, wo_ref, mask_ref, column, field, gate, nat, perm, tiles, fa, fb, s_ref, oa, ob,
    ra_out, rb_out, rs_out, ra_in, rb_in, rs_in, ba_out, bb_out, ba_in, bb_in, left, right, part,
    load_sem, line, send_sem, recv_sem, on_send, on_recv,
):
    row, chip, core = place()
    index = row * PLANE + chip
    loads = [
        pltpu.make_async_copy(src, dst, load_sem.at[n])
        for n, (src, dst) in enumerate(((pair_hbm, pair_ref), (w_hbm, w_ref), (wo_hbm, wo_ref)))
    ]
    for load in loads:
        load.start()
    arrived = greet(line)
    sends = Sends()
    tile_masks(valid_ref, mask_ref)
    loads[0].wait()
    start_field(pair_ref, ids_ref, bias_ref, field, column)

    for d in range(2):
        ra, rb, rs, ba, bb = ((ra_out, rb_out, rs_out, ba_out, bb_out), (ra_in, rb_in, rs_in, ba_in, bb_in))[d]
        sem = [(send_sem.at[5 * d + n], recv_sem.at[5 * d + n]) for n in range(5)]
        if d == 0:
            f_core, f_slot, s_slot = row % 2, (core, chip, row // 2), (core, chip, row)
        else:
            f_core, f_slot, s_slot = core, (row, chip), (core, row, chip)
        arrange(field, nat, perm, d == 1)
        if d == 0:
            arrived()
            loads[1].wait()
        s_ref[...] = project(perm, w_ref[d, :, 256:512], mask_ref[d], tiles)
        if d == 0:
            pl.semaphore_wait(line, PLANE - 1)
        sends.to_chips(lambda n: s_ref.at[n], rs.at[s_slot], *sem[0], sends.core)
        first = project(perm, w_ref[d, :, :256], mask_ref[d], tiles)
        fa[...] = first[:, 0]
        fb[...] = first[:, 1]
        f_to = sends.core if d == 1 else f_core
        sends.to_chips(lambda n: fa.at[n], ra.at[f_slot], *sem[1], f_to)
        project_gate(perm, w_ref[d, :, 512:], gate, d == 1)
        wait_bytes(rs.at[0], sem[0][1])
        copy_s = to_sibling(rs.at[core], on_send.at[d], on_recv.at[d])
        sends.to_chips(lambda n: fb.at[n], rb.at[f_slot], *sem[2], f_to)
        copy_s.wait()
        if d == 0:
            load_n = lambda k: rs[core if k < 8 else 1 - core, k % 8]
            load_a = lambda k: ra[core if k < 8 else 1 - core, k % 8]
            load_b = lambda k: rb[core if k < 8 else 1 - core, k % 8]
        else:
            load_n = lambda k: jnp.stack([rs[n % 2, k, n // 2] for n in range(16)], axis=0)
            load_a = lambda k: ra[k]
            load_b = lambda k: rb[k]
        assemble_right(load_n, right, part)
        wait_bytes(ra, sem[1][1])
        multiply(load_a, 0, left, right, oa)
        sends.to_owners(oa, ba.at[index], *sem[3])
        wait_bytes(rb, sem[2][1])
        multiply(load_b, 1, left, right, ob)
        sends.to_owners(ob, bb.at[index], *sem[4])
        if d == 0:
            loads[2].wait()
        wait_bytes(ba, sem[3][1])
        finish(field, gate, ba, wo_ref[d], tiles, 0)
        wait_bytes(bb, sem[4][1])
        finish(field, gate, bb, wo_ref[d], tiles, 1)
        sends.sent(s_ref, sem[0][0], False)
        sends.sent(fa, sem[1][0], d == 0)
        sends.sent(fb, sem[2][0], d == 0)
        sends.sent(ba, sem[3][0], True)
        sends.sent(bb, sem[4][0], True)
    for i in range(TOK):
        out_ref[i] = field[pl.ds(i * TOK, TOK)].astype(BF)


def per_device(pair, token_mask, chain_ids, chain_bias, in_weights, out_weights):
    hbm = pl.BlockSpec(memory_space=pl.ANY)
    smem = pl.BlockSpec(memory_space=pltpu.SMEM)
    vmem = pl.BlockSpec(memory_space=pltpu.VMEM)
    dma = pltpu.SemaphoreType.DMA
    tokens = pltpu.VMEM((TOK * TOK, CH), F32)
    half = lambda *dims: pltpu.VMEM(dims + (8, 128), BF)
    return pl.pallas_call(
        kernel,
        out_shape=jax.ShapeDtypeStruct((TOK, TOK, CH), BF),
        in_specs=[hbm, smem, smem, vmem, hbm, hbm],
        out_specs=vmem,
        scratch_shapes=[
            pltpu.VMEM((TOK, TOK, CH), BF),
            pltpu.VMEM((2, CH, 5 * CH), BF),
            pltpu.VMEM((2, CH, CH), BF),
            pltpu.VMEM((2, 16, 128), F32),
            pltpu.VMEM((TOK, CH), jnp.int32),
            tokens,
            tokens,
            tokens,
            pltpu.VMEM((PERM, CH), F32),
            pltpu.VMEM((PERM, CH), F32),
            half(CH),
            half(CH),
            half(CH, 2),
            half(16, 8),
            half(16, 8),
            half(2, 8, 8),
            half(2, 8, 8),
            half(2, 8, 16, 2),
            half(16, 8),
            half(16, 8),
            half(2, 16, 8, 2),
            half(CH),
            half(CH),
            half(CH),
            half(CH),
            pltpu.VMEM((192, 768), BF),
            pltpu.VMEM((768, 768), BF),
            pltpu.VMEM((768, 128), F32),
            dma((3,)),
            pltpu.SemaphoreType.REGULAR,
            dma((10,)),
            dma((10,)),
            dma((2,)),
            dma((2,)),
        ],
        compiler_params=pltpu.CompilerParams(
            collective_id=0, has_side_effects=True, vmem_limit_bytes=VMEM_LIMIT
        ),
        cost_estimate=pl.CostEstimate(flops=10**9, bytes_accessed=2 * 10**6, transcendentals=10**6),
        name="pairformer",
    )(pair, token_mask, chain_ids, chain_bias.reshape(1, CH), in_weights, out_weights)


def solution(mesh):
    return jax.shard_map(
        per_device,
        mesh=mesh,
        in_specs=(P("row", "col", None), P(), P(), P(), P(), P()),
        out_specs=P("row", "col", None),
        check_vma=False,
    )
```

time: 106 us -> 96.3 us (0.908)
  Pallas kernels: 104 us -> 94.4 us
    pallas_call x1, Pallas kernels: 104 us -> 94.4 us  [per_device(): pl.pallas_call(kernel, out_shape=jax.ShapeDtypeStruct((TOK, TOK, CH), BF)...]
where the time goes in v4:
time: 96.3 us; the launch traced here: 96.2 us
  Pallas kernels  94.4 us (98%)
  local copies, waits for them, and re-layouts  1.79 us (2%)
    pallas_call x1, Pallas kernels, per_device(): pl.pallas_call(kernel, out_shape=jax.ShapeDtypeStruct((TOK, TOK, CH), BF)...  94.4 us

profile of v4, /device:TPU:1, one launch (start us, length us, event | category | flops | bytes accessed | tf_op | source)
XLA Modules:
  0.0 96.2 jit_solution(15732708752777325366)
XLA Ops:
  0.0 94.4 %pairformer.1 = bf16[40,40,128]{2,1,0:T(8,128)(2,1)} custom-call(bf16[40,40,128]{2,1,0:T(8,128)(2,1)} %pair_hbm.1, s32[640]{0:T(1024)} %valid_ref.1, s32[640]{0:T(1024)} %ids_ref.1, f32[1,128]{1,0:T(1,128)} %bitcast.1, bf16[2,128,640]{2,1,0:T(8,128)(2,1)} %w_hbm.1, bf16[2,128,128]{2,1,0:T(8,128)(2,1)} %wo_hbm.1), custom_call_target="tpu_custom_call" | custom-call | flops 1000000000 | bytes 2000000 | tf_op jit(solution)/shard_map/pairformer/pallas_call | solution.py:376
  94.4 1.8 %copy.8 = bf16[40,40,128]{2,1,0:T(8,128)(2,1)} copy(bf16[40,40,128]{2,1,0:T(8,128)(2,1)} %pairformer.1) | data formatting | bytes 819200

commit v5 on v4

--- a/solution.py
+++ b/solution.py
@@ -12,7 +12,9 @@
 PLANE = 8
 CHIPS = ROWS * PLANE
 CH = 128
-PERM = 16 * 128
+DEPTH = 14
+PERM = DEPTH * 128
+HALVES = ((0, 8), (8, 6))
 BF = jnp.bfloat16
 F32 = jnp.float32
 VMEM_LIMIT = 60 * 2**20
@@ -53,17 +55,17 @@
         along = jnp.zeros((1, 128), F32)
         for b in range(TOK):
             along = jnp.where(place_b == b, b_valid[b], along)
-        for g in range(16):
-            low = jnp.where(third == 0, a_valid[g], a_valid[16 + g])
-            high = a_valid[32 + g] if 32 + g < TOK else 0.0
+        for g in range(DEPTH):
+            low = jnp.where(third == 0, a_valid[g], a_valid[DEPTH + g])
+            high = a_valid[2 * DEPTH + g] if 2 * DEPTH + g < TOK else 0.0
             mask[d, g : g + 1, :] = jnp.where(third == 2, high, low) * along
 
 
 def arrange(field_ref, nat, perm, swap):
     nat[...] = norm_lanes(field_ref[...])
-    for g in range(16):
+    for g in range(DEPTH):
         for q in range(3):
-            a = 16 * q + g
+            a = DEPTH * q + g
             at = pl.ds(g * 128 + TOK * q, TOK)
             if a >= TOK:
                 perm[at] = jnp.zeros((TOK, CH), F32)
@@ -76,23 +78,25 @@
 
 def project(perm, w, mask, tiles):
     weights_t = jnp.transpose(w.astype(F32)).astype(BF)
-    for part in range(4):
-        normed = perm[pl.ds(part * 512, 512)].astype(BF)
+    for lo in range(0, DEPTH, 4):
+        count = min(4, DEPTH - lo)
+        normed = perm[pl.ds(lo * 128, count * 128)].astype(BF)
         both = lax.dot_general(weights_t, normed, (((1,), (1,)), ((), ())), preferred_element_type=F32)
         value = sigmoid(both[:CH]) * both[CH:]
-        for n in range(4):
-            g = part * 4 + n
-            tiles[pl.ds(g, CH, stride=16)] = value[:, n * 128 : n * 128 + 128] * mask[g : g + 1, :]
-    return tiles[...].reshape(CH, 2, 8, 128).astype(BF)
+        for n in range(count):
+            g = lo + n
+            tiles[pl.ds(g, CH, stride=DEPTH)] = value[:, n * 128 : n * 128 + 128] * mask[g : g + 1, :]
+    return tiles[pl.ds(0, CH * DEPTH)].astype(BF).reshape(CH, 7, 2, 128)
 
 
 def project_gate(perm, w, gate_ref, swap):
-    for part in range(4):
-        normed = perm[pl.ds(part * 512, 512)].astype(BF)
+    for lo in range(0, DEPTH, 4):
+        count = min(4, DEPTH - lo)
+        normed = perm[pl.ds(lo * 128, count * 128)].astype(BF)
         value = sigmoid(jnp.dot(normed, w, preferred_element_type=F32))
-        for n in range(4):
+        for n in range(count):
             for q in range(3):
-                a = 16 * q + part * 4 + n
+                a = DEPTH * q + lo + n
                 if a < TOK:
                     piece = value[n * 128 + q * TOK : n * 128 + q * TOK + TOK]
                     if swap:
@@ -102,17 +106,19 @@
 
 
 def finish(field_ref, gate_ref, r_ref, weights, tiles, half):
-    x = r_ref[...].astype(F32)
+    lo, depth = HALVES[half]
+    x = r_ref[...].astype(F32).reshape(CH, depth, 128)
     center = x - jnp.mean(x, axis=0, keepdims=True)
     spread = jnp.mean(center * center, axis=0, keepdims=True)
-    tiles[pl.ds(0, CH * 8)] = (center * lax.rsqrt(spread + 1e-05)).reshape(CH * 8, 128)
-    for g in range(8):
-        normed = tiles[pl.ds(g, CH, stride=8)].astype(BF)
+    tiles[pl.ds(0, CH * depth)] = (center * lax.rsqrt(spread + 1e-05)).reshape(CH * depth, 128)
+    for g in range(depth):
+        normed = tiles[pl.ds(g, CH, stride=depth)].astype(BF)
         out = lax.dot_general(normed, weights, (((0,), (0,)), ((), ())), preferred_element_type=F32)
-        for q in range(3 - half):
-            a = 16 * q + 8 * half + g
-            at = pl.ds(a * TOK, TOK)
-            field_ref[at] = field_ref[at] + gate_ref[at] * out[q * TOK : q * TOK + TOK]
+        for q in range(3):
+            a = DEPTH * q + lo + g
+            if a < TOK:
+                at = pl.ds(a * TOK, TOK)
+                field_ref[at] = field_ref[at] + gate_ref[at] * out[q * TOK : q * TOK + TOK]
 
 
 def lanes_between(lo, hi, rows):
@@ -135,32 +141,34 @@
 def assemble_right(load_n, right, part):
     part[...] = jnp.zeros((768, 128), F32)
     for group, blocks in enumerate(GROUPS):
-        parts = [load_n(k).astype(F32).reshape(256, 128) for k in blocks]
+        parts = [load_n(k).astype(F32).reshape(16 * DEPTH, 128) for k in blocks]
         for q in range(3):
-            value = spread_lanes(parts, q, 256)
+            value = spread_lanes(parts, q, 16 * DEPTH)
             for n in range(16):
-                depth = 16 if q < 2 else 8
-                part[pl.ds(128 * (n // 3) + TOK * (n % 3) + 16 * q, depth)] = value[n * 16 : n * 16 + depth]
+                depth = min(DEPTH, TOK - DEPTH * q)
+                at = pl.ds(128 * (n // 3) + TOK * (n % 3) + DEPTH * q, depth)
+                part[at] = value[n * DEPTH : n * DEPTH + depth]
         right[:, pl.ds(group * 128, 128)] = part[...].astype(BF)
 
 
 def multiply(load_m, half, left, right, out_ref):
+    size = 8 * HALVES[half][1]
     for group, blocks in enumerate(GROUPS):
-        parts = [load_m(k).astype(F32).reshape(64, 128) for k in blocks]
-        for q in range(3 - half):
-            left[pl.ds(q * 64, 64), pl.ds(group * 128, 128)] = spread_lanes(parts, q, 64).astype(BF)
-    rows = left[pl.ds(0, 64 * (3 - half))]
+        parts = [load_m(k).astype(F32).reshape(size, 128) for k in blocks]
+        for q in range(3):
+            left[pl.ds(q * size, size), pl.ds(group * 128, 128)] = spread_lanes(parts, q, size).astype(BF)
+    rows = left[pl.ds(0, 3 * size)]
     total = lax.dot_general(rows, right[...], (((1,), (1,)), ((), ())), preferred_element_type=F32)
     for n in range(16):
         n3, m = n // 3, n % 3
-        value = jnp.zeros((64, 128), F32)
-        for q in range(3 - half):
+        value = jnp.zeros((size, 128), F32)
+        for q in range(3):
             value = jnp.where(
-                lanes_between(TOK * q, TOK * q + TOK, 64),
-                roll(total[q * 64 : q * 64 + 64, n3 * 128 : n3 * 128 + 128], TOK * (q - m)),
+                lanes_between(TOK * q, TOK * q + TOK, size),
+                roll(total[q * size : q * size + size, n3 * 128 : n3 * 128 + 128], TOK * (q - m)),
                 value,
             )
-        out_ref[n] = value.reshape(8, 8, 128).astype(BF)
+        out_ref[n] = value.astype(BF).reshape(8, size // 16, 2, 128)
 
 
 def place():
@@ -327,8 +335,8 @@
             pl.semaphore_wait(line, PLANE - 1)
         sends.to_chips(lambda n: s_ref.at[n], rs.at[s_slot], *sem[0], sends.core)
         first = project(perm, w_ref[d, :, :256], mask_ref[d], tiles)
-        fa[...] = first[:, 0]
-        fb[...] = first[:, 1]
+        fa[...] = first[:, :4]
+        fb[...] = first[:, 4:]
         f_to = sends.core if d == 1 else f_core
         sends.to_chips(lambda n: fa.at[n], ra.at[f_slot], *sem[1], f_to)
         project_gate(perm, w_ref[d, :, 512:], gate, d == 1)
@@ -372,7 +380,8 @@
     vmem = pl.BlockSpec(memory_space=pltpu.VMEM)
     dma = pltpu.SemaphoreType.DMA
     tokens = pltpu.VMEM((TOK * TOK, CH), F32)
-    half = lambda *dims: pltpu.VMEM(dims + (8, 128), BF)
+    pairs = lambda count, *dims: pltpu.VMEM(dims + (count, 2, 128), BF)
+    low, high, whole = (lambda *dims, count=count: pairs(count, *dims) for count in (4, 3, 7))
     return pl.pallas_call(
         kernel,
         out_shape=jax.ShapeDtypeStruct((TOK, TOK, CH), BF),
@@ -389,21 +398,21 @@
             tokens,
             pltpu.VMEM((PERM, CH), F32),
             pltpu.VMEM((PERM, CH), F32),
-            half(CH),
-            half(CH),
-            half(CH, 2),
-            half(16, 8),
-            half(16, 8),
-            half(2, 8, 8),
-            half(2, 8, 8),
-            half(2, 8, 16, 2),
-            half(16, 8),
-            half(16, 8),
-            half(2, 16, 8, 2),
-            half(CH),
-            half(CH),
-            half(CH),
-            half(CH),
+            low(CH),
+            high(CH),
+            whole(CH),
+            low(16, 8),
+            high(16, 8),
+            low(2, 8, 8),
+            high(2, 8, 8),
+            whole(2, 8, 16),
+            low(16, 8),
+            high(16, 8),
+            whole(2, 16, 8),
+            low(CH),
+            high(CH),
+            low(CH),
+            high(CH),
             pltpu.VMEM((192, 768), BF),
             pltpu.VMEM((768, 768), BF),
             pltpu.VMEM((768, 128), F32),

time: 96.3 us -> 90.6 us (0.941)
  Pallas kernels: 94.4 us -> 88.6 us
    pallas_call x1, Pallas kernels: 94.4 us -> 88.6 us  [per_device(): pl.pallas_call(kernel, out_shape=jax.ShapeDtypeStruct((TOK, TOK, CH), BF)...]
where the time goes in v5:
time: 90.6 us; the launch traced here: 90.4 us
  Pallas kernels  88.6 us (98%)
  local copies, waits for them, and re-layouts  1.79 us (2%)
    pallas_call x1, Pallas kernels, per_device(): pl.pallas_call(kernel, out_shape=jax.ShapeDtypeStruct((TOK, TOK, CH), BF)...  88.6 us

profile of v5, /device:TPU:1, one launch (start us, length us, event | category | flops | bytes accessed | tf_op | source)
XLA Modules:
  0.0 90.4 jit_solution(11314126795132408282)
XLA Ops:
  0.0 88.6 %pairformer.1 = bf16[40,40,128]{2,1,0:T(8,128)(2,1)} custom-call(bf16[40,40,128]{2,1,0:T(8,128)(2,1)} %pair_hbm.1, s32[640]{0:T(1024)} %valid_ref.1, s32[640]{0:T(1024)} %ids_ref.1, f32[1,128]{1,0:T(1,128)} %bitcast.1, bf16[2,128,640]{2,1,0:T(8,128)(2,1)} %w_hbm.1, bf16[2,128,128]{2,1,0:T(8,128)(2,1)} %wo_hbm.1), custom_call_target="tpu_custom_call" | custom-call | flops 1000000000 | bytes 2000000 | tf_op jit(solution)/shard_map/pairformer/pallas_call | solution.py:385
  88.6 1.8 %copy.8 = bf16[40,40,128]{2,1,0:T(8,128)(2,1)} copy(bf16[40,40,128]{2,1,0:T(8,128)(2,1)} %pairformer.1) | data formatting | bytes 819200

commit v6 on v5

--- a/solution.py
+++ b/solution.py
@@ -138,17 +138,17 @@
     return total
 
 
-def assemble_right(load_n, right, part):
-    part[...] = jnp.zeros((768, 128), F32)
-    for group, blocks in enumerate(GROUPS):
-        parts = [load_n(k).astype(F32).reshape(16 * DEPTH, 128) for k in blocks]
+def assemble_right(load_n, groups, blocks_n, rows, right, part):
+    size = len(blocks_n) * DEPTH
+    for group in groups:
+        parts = [load_n(k).astype(F32).reshape(size, 128) for k in GROUPS[group]]
         for q in range(3):
-            value = spread_lanes(parts, q, 16 * DEPTH)
-            for n in range(16):
+            value = spread_lanes(parts, q, size)
+            for place_n, n in enumerate(blocks_n):
                 depth = min(DEPTH, TOK - DEPTH * q)
                 at = pl.ds(128 * (n // 3) + TOK * (n % 3) + DEPTH * q, depth)
-                part[at] = value[n * DEPTH : n * DEPTH + depth]
-        right[:, pl.ds(group * 128, 128)] = part[...].astype(BF)
+                part[at] = value[place_n * DEPTH : place_n * DEPTH + depth]
+        right[rows, pl.ds(group * 128, 128)] = part[rows].astype(BF)
 
 
 def multiply(load_m, half, left, right, out_ref):
@@ -254,7 +254,7 @@
         def _():
             remote(src, dst, send_sem, recv_sem, to_row, to_col).start()
 
-    def to_owners(self, o_ref, dst, send_sem, recv_sem):
+    def to_owners(self, o_ref, slot, dst, send_sem, recv_sem):
         parity = self.row % 2
 
         def visit(x, dy, line):
@@ -262,7 +262,7 @@
                 to_row, to_chip = x * 4 + z_hi, self.y[dy] + z_lo
                 for other in (0, 1):
                     to_col = to_chip * 2 + (1 - self.core if other else self.core)
-                    src = o_ref.at[to_col, to_row // 2]
+                    src = o_ref.at[slot(to_chip, other, to_col), to_row // 2]
                     copy = remote(src, dst, send_sem, recv_sem, to_row, to_col)
                     if line and n == 1 and not other:
 
@@ -314,6 +314,7 @@
     for load in loads:
         load.start()
     arrived = greet(line)
+    part[...] = jnp.zeros((768, 128), F32)
     sends = Sends()
     tile_masks(valid_ref, mask_ref)
     loads[0].wait()
@@ -342,23 +343,27 @@
         project_gate(perm, w_ref[d, :, 512:], gate, d == 1)
         wait_bytes(rs.at[0], sem[0][1])
         copy_s = to_sibling(rs.at[core], on_send.at[d], on_recv.at[d])
+        if d == 0:
+            plane = lambda k: core if k < 8 else 1 - core
+            load_n = (lambda k: rs[plane(k), k % 8],) * 2
+            load_a, load_b = (lambda k: ra[plane(k), k % 8]), (lambda k: rb[plane(k), k % 8])
+            shares = ((range(3), range(16), pl.ds(0, 768)), (range(3, 6), range(16), pl.ds(0, 768)))
+            slot = lambda to_chip, other, to_col: to_col
+        else:
+            load_n = (lambda k: rs[core, k], lambda k: rs[1 - core, k])
+            load_a, load_b = (lambda k: ra[k]), (lambda k: rb[k])
+            shares = ((range(6), range(8), pl.ds(0, 336)), (range(6), range(8, 16), pl.ds(336, 432)))
+            slot = lambda to_chip, other, to_col: other * 8 + to_chip
+        assemble_right(load_n[0], *shares[0], right, part)
         sends.to_chips(lambda n: fb.at[n], rb.at[f_slot], *sem[2], f_to)
         copy_s.wait()
-        if d == 0:
-            load_n = lambda k: rs[core if k < 8 else 1 - core, k % 8]
-            load_a = lambda k: ra[core if k < 8 else 1 - core, k % 8]
-            load_b = lambda k: rb[core if k < 8 else 1 - core, k % 8]
-        else:
-            load_n = lambda k: jnp.stack([rs[n % 2, k, n // 2] for n in range(16)], axis=0)
-            load_a = lambda k: ra[k]
-            load_b = lambda k: rb[k]
-        assemble_right(load_n, right, part)
+        assemble_right(load_n[1], *shares[1], right, part)
         wait_bytes(ra, sem[1][1])
         multiply(load_a, 0, left, right, oa)
-        sends.to_owners(oa, ba.at[index], *sem[3])
+        sends.to_owners(oa, slot, ba.at[index], *sem[3])
         wait_bytes(rb, sem[2][1])
         multiply(load_b, 1, left, right, ob)
-        sends.to_owners(ob, bb.at[index], *sem[4])
+        sends.to_owners(ob, slot, bb.at[index], *sem[4])
         if d == 0:
             loads[2].wait()
         wait_bytes(ba, sem[3][1])

time: 90.6 us -> 90.5 us (level)
  no operation moved by 1% of the time
where the time goes in v6:
time: 90.5 us; the launch traced here: 90.3 us
  Pallas kernels  88.5 us (98%)
  local copies, waits for them, and re-layouts  1.79 us (2%)
    pallas_call x1, Pallas kernels, per_device(): pl.pallas_call(kernel, out_shape=jax.ShapeDtypeStruct((TOK, TOK, CH), BF)...  88.5 us

profile of v6, /device:TPU:1, one launch (start us, length us, event | category | flops | bytes accessed | tf_op | source)
XLA Modules:
  0.0 90.3 jit_solution(16337944698900728245)
XLA Ops:
  0.0 88.5 %pairformer.1 = bf16[40,40,128]{2,1,0:T(8,128)(2,1)} custom-call(bf16[40,40,128]{2,1,0:T(8,128)(2,1)} %pair_hbm.1, s32[640]{0:T(1024)} %valid_ref.1, s32[640]{0:T(1024)} %ids_ref.1, f32[1,128]{1,0:T(1,128)} %bitcast.1, bf16[2,128,640]{2,1,0:T(8,128)(2,1)} %w_hbm.1, bf16[2,128,128]{2,1,0:T(8,128)(2,1)} %wo_hbm.1), custom_call_target="tpu_custom_call" | custom-call | flops 1000000000 | bytes 2000000 | tf_op jit(solution)/shard_map/pairformer/pallas_call | solution.py:390
  88.5 1.8 %copy.8 = bf16[40,40,128]{2,1,0:T(8,128)(2,1)} copy(bf16[40,40,128]{2,1,0:T(8,128)(2,1)} %pairformer.1) | data formatting | bytes 819200
